TPU v7x, 256 devices: a whole 4x4x8 slice. The times are simulated.
256 devices in a mesh: group: 8 (over z_lo, y), fsdp: 32 (over z_hi, x, core).
Axes of the slice: x: 4, y: 4, z: 8 (z_hi: 4, z_lo: 2; z = z_hi * 2 + z_lo), core: 2. Of those that a mesh axis runs over, the one named last changes fastest.
Arguments:
- inner_weights: float32 [8, 2048, 7168], P('group', 'fsdp'), may hold values from -0.125 to 0.125
- inner_grads: bfloat16 [8, 2048, 7168], P('group', 'fsdp'), may hold values from -6 to 6
- first_moment: float32 [8, 2048, 7168], P('group', 'fsdp'), may hold values from -0.6 to 0.6
- second_moment: float32 [8, 2048, 7168], P('group', 'fsdp'), may hold values from 0.01 to 0.25
- anchor: float32 [2048, 7, 1024], P('fsdp'), may hold values from -0.125 to 0.125
- outer_momentum: float32 [2048, 7, 1024], P('fsdp', None, 'group'), may hold values from -0.06 to 0.06
- next_tokens: bfloat16 [49152, 2048], P(('group', 'fsdp')), may hold values from -6 to 6
Outputs:
- preactivations: bfloat16 [49152, 7168], P(('group', 'fsdp'))
- new_anchor: float32 [2048, 7, 1024], P('fsdp', None, 'group')
- new_momentum: float32 [2048, 7, 1024], P('fsdp', None, 'group')
All inputs are finite; a program needn't handle non-finite values.
Results may differ from a plain program's by a relative error of at most 0.0049.
Values may be sent and summed in bfloat16 or wider, within the bound.
No kernel may reach another device: no remote copies, remote signals or barrier semaphores. Data moves between devices by JAX's collectives and lax.ppermute only.
A program may use at most 128 MiB of HBM per device.

v0:
```python
import jax
import jax.numpy as jnp
from jax import lax
from jax.sharding import PartitionSpec as P

INNER_STEPS = 100


first_decay = 0.9
second_decay = 0.95
inner_rate = 0.04
weight_decay = 0.1
epsilon = 1e-08
momentum_decay = 0.9
outer_rate = 0.7
mixing = 0.5


def adam_step(weights, gradient, moment_one, moment_two):
    gradient = gradient.astype(jnp.float32)
    first_new = first_decay * moment_one + (1.0 - first_decay) * gradient
    second_new = second_decay * moment_two + (1.0 - second_decay) * gradient * gradient
    correct_one = 1.0 - first_decay**INNER_STEPS
    correct_two = 1.0 - second_decay**INNER_STEPS
    update = first_new / correct_one / (jnp.sqrt(second_new / correct_two) + epsilon)
    return weights - inner_rate * (update + weight_decay * weights)


def outer_update(summed, anchor_part, momentum_part, groups):
    mean_delta = summed / groups
    momentum_new = momentum_decay * momentum_part + mean_delta
    anchor_new = anchor_part - outer_rate * (mean_delta + momentum_decay * momentum_new)
    return (anchor_new, momentum_new)


def body(
    inner_weights, inner_grads, first_moment, second_moment, anchor, outer_momentum, next_tokens
):
    groups = lax.axis_size("group")
    share_width = outer_momentum.shape[2]
    offset = lax.axis_index("group") * share_width
    inner_new = adam_step(inner_weights[0], inner_grads[0], first_moment[0], second_moment[0])
    inner_cube = inner_new.reshape(anchor.shape)
    pseudo = anchor - inner_cube
    summed = lax.psum_scatter(pseudo, "group", scatter_dimension=2, tiled=True)
    anchor_part = lax.dynamic_slice_in_dim(anchor, offset, share_width, 2)
    anchor_new, momentum_new = outer_update(summed, anchor_part, outer_momentum, groups)
    anchor_full = lax.all_gather(anchor_new, "group", axis=2, tiled=True)
    mixed_cube = (mixing * inner_cube + (1.0 - mixing) * anchor_full).astype(jnp.bfloat16)
    mixed_matrix = mixed_cube.reshape(inner_new.shape)
    product = jnp.dot(
        next_tokens,
        lax.all_gather(mixed_matrix, "fsdp", axis=0, tiled=True),
        preferred_element_type=jnp.float32,
    )
    preactivations = product.astype(jnp.bfloat16)
    return (preactivations, anchor_new, momentum_new)


def solution(mesh):
    in_specs = (
        P("group", "fsdp", None),
        P("group", "fsdp", None),
        P("group", "fsdp", None),
        P("group", "fsdp", None),
        P("fsdp", None, None),
        P("fsdp", None, "group"),
        P(("group", "fsdp"), None),
    )
    out_specs = (P(("group", "fsdp"), None), P("fsdp", None, "group"), P("fsdp", None, "group"))
    return jax.shard_map(body, mesh=mesh, in_specs=in_specs, out_specs=out_specs, check_vma=False)
```

profile of v0, /device:TPU:1, one launch (start us, length us, event | category | flops | bytes accessed | tf_op | source)
XLA Modules:
  0.0 335.9 jit_solution(9067732433899380768)
XLA Ops:
  7.2 0.0 copy-start
  7.2 0.0 reduce-scatter.2.cloned.1.call-start
  7.2 1.7 broadcast_multiply_fusion.1
  9.0 2.3 mul.67
  11.2 1.7 broadcast_multiply_fusion
  12.9 2.3 mul.71
  15.2 0.0 copy-start.2
  15.2 3.2 squeeze.2
  18.4 0.0 copy-done.2
  18.4 2.4 reshape.21
  20.8 8.4 %copy_subtract_fusion = (f32[64,7,1024]{2,1,0:T(8,128)}, f32[64,7,1024]{2,1,0:T(8,128)S(1)}, f32[64,7,1024]{2,1,0:T(8,128)}) fusion(f32[64,7,1024]{2,0,1:T(8,128)} %param.11, f32[64,7,1024]{2,1,0:T(8,128)} %squeeze.2, f32[64,7,1024]{2,1,0:T(8,128)} %mul.71, f32[64,7,1024]{2,1,0:T(8,128)} %reshape.21, f32[64,7,1024]{2,1,0:T(8,128)} %mul.67), kind=kLoop, calls=%fused_computation.16 | loop fusion | flops 6422528 | bytes 14680064 | tf_op jit(solution)/shard_map/sub | solution.py:44
  29.2 0.0 copy-start.3
  29.2 0.0 reduce-scatter.2.cloned.1.call-update
  29.3 0.0 all-gather.3.cloned.1.call-start
  29.3 43.9 %reduce-scatter.2.cloned.1.call-done = f32[64,7,128]{2,1,0:T(8,128)} async-done(((f32[64,7,1024]{2,1,0:T(8,128)}), f32[64,7,128]{2,1,0:T(8,128)}) %reduce-scatter.2.cloned.1.call-update) | async-done | bytes 229392 | tf_op jit(solution)/shard_map/reduce_scatter | solution.py:45
  73.3 0.0 copy-done.3
  73.3 1.9 fusion.7
  75.2 0.0 all-gather.3.cloned.1.call-update
  75.2 0.0 all-gather.5.cloned.1.call-start
  75.3 47.9 %all-gather.3.cloned.1.call-done = f32[64,7,1024]{2,1,0:T(8,128)} async-done(((f32[64,7,128]{2,1,0:T(8,128)}), f32[64,7,1024]{2,1,0:T(8,128)}) %all-gather.3.cloned.1.call-update) | async-done | bytes 1835024 | tf_op jit(solution)/shard_map/all_gather | solution.py:48
  123.2 2.0 multiply_convert_fusion
  125.1 0.0 copy-start.1
  125.1 1.5 copy.15
  126.7 0.0 all-gather.5.cloned.1.call-update
  126.7 0.0 copy-done.1
  126.7 0.7 copy.13
  127.4 0.7 copy.14
  128.2 186.9 %all-gather.5.cloned.1.call-done = bf16[2048,7168]{1,0:T(8,128)(2,1)} async-done(((bf16[64,7168]{1,0:T(8,128)(2,1)}), bf16[2048,7168]{1,0:T(8,128)(2,1)}) %all-gather.5.cloned.1.call-update) | async-done | bytes 29360144 | tf_op jit(solution)/shard_map/all_gather | solution.py:53
  315.1 0.0 copy-done
  315.1 14.3 %fusion = bf16[192,7168]{1,0:T(8,128)(2,1)} fusion(bf16[192,2048]{1,0:T(8,128)(2,1)S(1)} %copy-done, bf16[2048,7168]{1,0:T(8,128)(2,1)} %all-gather.5.cloned.1.call-done), kind=kOutput, calls=%fused_computation.1 | convolution fusion | flops 5638520832 | bytes 32899072 | tf_op jit(solution)/shard_map/dot_general | solution.py:51
Async XLA Ops:
  7.2 307.9 %copy-start = (bf16[192,2048]{1,0:T(8,128)(2,1)S(1)}, bf16[192,2048]{1,0:T(8,128)(2,1)}, u32[]{:S(2)}) copy-start(bf16[192,2048]{1,0:T(8,128)(2,1)} %param.13) | copy-start | bytes 2359300
  7.2 66.1 %reduce-scatter.2.cloned.1.call-start = ((), (), s32[]{:S(2)}) async-start(), calls=%async_computation.1 | async-start | bytes 2359296 | tf_op jit(solution)/shard_map/reduce_scatter | solution.py:45
  15.2 3.3 copy-start.2
  29.2 44.0 %copy-start.3 = (f32[64,7,128]{2,0,1:T(8,128)S(1)}, f32[64,7,128]{2,0,1:T(8,128)}, u32[]{:S(2)}) copy-start(f32[64,7,128]{2,0,1:T(8,128)} %param.12) | copy-start | bytes 688132
  29.3 93.9 %all-gather.3.cloned.1.call-start = ((), (), s32[]{:S(2)}) async-start(), calls=%async_computation.2 | async-start | bytes 2359296 | tf_op jit(solution)/shard_map/all_gather | solution.py:48
  75.2 239.9 %all-gather.5.cloned.1.call-start = ((), (), s32[]{:S(2)}) async-start(), calls=%async_computation.3 | async-start | bytes 30277632 | tf_op jit(solution)/shard_map/all_gather | solution.py:53
  125.1 1.6 copy-start.1
Sparse Core Ops, SparseCore 0:
  29.4 43.8 reduce-scatter.1
  75.3 47.7 all-gather.2
  126.8 188.2 all-gather.4
where the time goes:
time: 336 us
  waiting for transfers between devices  279 us (83%)
  other arithmetic  15.7 us (5%)
  matrix products  14.3 us (4%)
  between operations  13.8 us (4%)
  local copies, waits for them, and re-layouts  13.2 us (4%)
    all_gather x1, waiting for transfers between devices, body(): lax.all_gather(mixed_matrix, 'fsdp', axis=0, tiled=True)  187 us
    all_gather x1, waiting for transfers between devices, body(): anchor_full = lax.all_gather(anchor_new, 'group', axis=2, tiled=True)  47.9 us
    reduce_scatter x1, waiting for transfers between devices, body(): summed = lax.psum_scatter(pseudo, 'group', scatter_dimension=2, tiled=True)  43.9 us
    dot_general x1, matrix products, body(): jnp.dot(next_tokens, lax.all_gather(mixed_matrix, 'fsdp', axis=0, tiled=T...  14.3 us
    sub x1, other arithmetic, body(): pseudo = anchor - inner_cube  8.41 us
  transfers between devices with their start and end apart: 3, of which 3 were waited for; matrix products, arithmetic and copies ran while one was open for 0% of the time, Pallas kernels for 0%

commit v1 on v0

v1 whole, which is shorter than its diff:
```python
import jax
import jax.numpy as jnp
from jax import lax
from jax.experimental import pallas as pl
from jax.experimental.pallas import tpu as pltpu
from jax.sharding import Mesh
from jax.sharding import PartitionSpec as P

INNER_STEPS = 100

first_decay = 0.9
second_decay = 0.95
inner_rate = 0.04
weight_decay = 0.1
epsilon = 1e-08
momentum_decay = 0.9
outer_rate = 0.7
mixing = 0.5

GROUP = ("zl", "y")
ROWS = ("zh", "x", "c")
PLANE = ("x", "c")
SLICES = 7
LANES = 128
CHUNKS = ((0, 4), (4, 7))
BRIEF = pl.CostEstimate(flops=1, bytes_accessed=1, transcendentals=0)


def adam_step(weights, gradient, moment_one, moment_two):
    gradient = gradient.astype(jnp.float32)
    first_new = first_decay * moment_one + (1.0 - first_decay) * gradient
    second_new = second_decay * moment_two + (1.0 - second_decay) * gradient * gradient
    correct_one = 1.0 - first_decay**INNER_STEPS
    correct_two = 1.0 - second_decay**INNER_STEPS
    update = first_new / correct_one / (jnp.sqrt(second_new / correct_two) + epsilon)
    return weights - inner_rate * (update + weight_decay * weights)


def inner_kernel(weights, grads, moment_one, moment_two, anchor, pieces):
    inner_new = adam_step(weights[...], grads[...], moment_one[...], moment_two[...])
    pseudo = (anchor[0] - inner_new).astype(jnp.bfloat16)
    for g in range(pieces.shape[0]):
        pieces[g] = pseudo[:, g * LANES : (g + 1) * LANES]


def inner_step(weights, grads, moment_one, moment_two, anchor, groups):
    rows, width = weights.shape[0], anchor.shape[2]
    wide = pl.BlockSpec((rows, width), lambda s: (0, s))
    return pl.pallas_call(
        inner_kernel,
        grid=(SLICES,),
        in_specs=[wide] * 4 + [pl.BlockSpec((1, rows, width), lambda s: (s, 0, 0))],
        out_specs=pl.BlockSpec((groups, rows, LANES), lambda s: (0, 0, s)),
        out_shape=jax.ShapeDtypeStruct((groups, rows, SLICES * LANES), jnp.bfloat16),
        compiler_params=pltpu.CompilerParams(vmem_limit_bytes=60 * 1024 * 1024),
        cost_estimate=BRIEF,
    )(weights, grads, moment_one, moment_two, anchor)


def outer_kernel(place, pieces, anchor, momentum, anchor_new, momentum_new, *mixed):
    groups = pieces.shape[0]
    pseudo = [pieces[g].astype(jnp.float32) for g in range(groups)]
    mean_delta = sum(pseudo[1:], pseudo[0]) / groups
    after = momentum_decay * momentum[0] + mean_delta
    moved = anchor[0] - outer_rate * (mean_delta + momentum_decay * after)
    momentum_new[0] = after
    anchor_new[0] = moved
    s = pl.program_id(0)
    for (first, last), part in zip(CHUNKS, mixed):

        @pl.when((s >= first) & (s < last))
        def _():
            for g in range(groups):
                inner_new = anchor[0] - pseudo[g]
                part[g] = (mixing * inner_new + (1.0 - mixing) * moved).astype(jnp.bfloat16)


def outer_step(place, pieces, anchor, momentum):
    groups, rows, _ = pieces.shape
    part = pl.BlockSpec((1, rows, LANES), lambda s, p: (s, 0, 0))
    anchor_part = pl.BlockSpec((1, rows, LANES), lambda s, p: (s, 0, p[0]))
    new = jax.ShapeDtypeStruct(momentum.shape, jnp.float32)

    def chunk(first, last):
        return pl.BlockSpec(
            (groups, rows, LANES), lambda s, p: (0, 0, jnp.clip(s - first, 0, last - first - 1))
        )

    return pl.pallas_call(
        outer_kernel,
        grid_spec=pltpu.PrefetchScalarGridSpec(
            num_scalar_prefetch=1,
            grid=(SLICES,),
            in_specs=[pl.BlockSpec((groups, rows, LANES), lambda s, p: (0, 0, s)), anchor_part, part],
            out_specs=[part, part] + [chunk(*c) for c in CHUNKS],
        ),
        out_shape=[new, new]
        + [
            jax.ShapeDtypeStruct((groups, rows, (last - first) * LANES), jnp.bfloat16)
            for first, last in CHUNKS
        ],
        cost_estimate=BRIEF,
    )(place, pieces, anchor, momentum)


def product_kernel(place, tokens, *refs):
    *weights, out = refs
    total = None
    for k, weight in enumerate(weights):
        depth = weight.shape[0]
        columns = pl.ds(pl.multiple_of(place[2 + k], depth), depth)
        term = jnp.dot(tokens[0, :, columns], weight[...], preferred_element_type=jnp.float32)
        total = term if total is None else total + term
    chips = out.shape[1]
    total = total.astype(jnp.bfloat16).reshape(chips, -1, out.shape[3])
    for k, step in enumerate((0, 3, 1, 2)):
        out[0, lax.rem(place[0] + step, chips)] = total[k]


def product(place, tokens, weights, cost):
    cores, rows, depth = tokens.shape
    chips = 4
    width = weights[0].shape[1]
    return pl.pallas_call(
        product_kernel,
        grid_spec=pltpu.PrefetchScalarGridSpec(
            num_scalar_prefetch=1,
            grid=(cores,),
            in_specs=[pl.BlockSpec((1, rows, depth), lambda d, p: (d, 0, 0))]
            + [pl.BlockSpec(w.shape, lambda d, p: (0, 0)) for w in weights],
            out_specs=pl.BlockSpec(
                (1, chips, rows // chips, width), lambda d, p: (p[1] ^ d, 0, 0, 0)
            ),
        ),
        out_shape=jax.ShapeDtypeStruct((cores, chips, rows // chips, width), jnp.bfloat16),
        compiler_params=pltpu.CompilerParams(vmem_limit_bytes=48 * 1024 * 1024),
        cost_estimate=cost,
    )(place, tokens, *weights)


def assemble_kernel(part, *refs):
    out = refs[-1]
    half = part.shape[0] // 2
    for j in range(2 * half):
        column = (2 * (j % half) + j // half) * LANES
        out[:, column : column + LANES] = part[j]


def assemble(part, whole, first, last):
    count, rows, _ = part.shape
    width = count * LANES
    held = [] if whole is None else [whole]
    return pl.pallas_call(
        assemble_kernel,
        grid=(last - first,),
        in_specs=[pl.BlockSpec((count, rows, LANES), lambda s: (0, 0, s))]
        + [pl.BlockSpec(memory_space=pl.ANY)] * len(held),
        out_specs=pl.BlockSpec((rows, width), lambda s: (0, s + first)),
        out_shape=jax.ShapeDtypeStruct((rows, SLICES * width), jnp.bfloat16),
        input_output_aliases={1: 0} if held else {},
        cost_estimate=BRIEF,
    )(part, *held)


def shift(array, axis, k):
    n = lax.axis_size(axis)
    return lax.ppermute(array, axis, [(i, (i + k) % n) for i in range(n)])


def neighbours(array, axis):
    return shift(array, axis, 1), shift(array, axis, -1)


def opposite(low, high, axis):
    half = low.shape[0] // 2
    return shift(low[:half], axis, 1), shift(high[half:], axis, -1)


def after(array, earlier):
    if earlier is None:
        return array
    return lax.optimization_barrier((array, earlier))[0]


def body(
    inner_weights, inner_grads, first_moment, second_moment, anchor, outer_momentum, next_tokens
):
    groups = lax.axis_size(GROUP)
    place = lax.axis_index(GROUP).astype(jnp.int32).reshape(1)
    deep = next_tokens.shape[1] // lax.axis_size("zh")
    z = [(lax.axis_index("zh") + k) % lax.axis_size("zh") * deep for k in (0, -1, 1, 2, 2)]
    z[4] = z[4] + deep // 2
    spot = jnp.stack([lax.axis_index("x"), lax.axis_index("c")] + z).astype(jnp.int32)
    anchor = anchor.transpose(1, 0, 2)
    momentum = outer_momentum.transpose(1, 0, 2)

    pieces = inner_step(
        inner_weights[0], inner_grads[0], first_moment[0], second_moment[0], anchor, groups
    )
    pieces = lax.all_to_all(pieces, GROUP, 0, 0, tiled=True)
    sides = neighbours(next_tokens, "x")
    anchor_new, momentum_new, *mixed = outer_step(place, after(pieces, sides), anchor, momentum)
    across = opposite(*sides, "x")

    weights, held = [], across
    for part in mixed:
        part = lax.all_to_all(part, GROUP, 0, 0, tiled=True)
        part = lax.all_to_all(after(part, held), PLANE, 0, 0, tiled=True)
        block = part.reshape(-1, part.shape[2])
        held = neighbours(block, "zh")
        weights.append((block, *held, *opposite(*held, "zh")))

    near = jnp.concatenate([next_tokens, *sides, *across])
    tokens = jnp.stack([near, shift(near, "c", 1)])
    preactivations = None
    for (first, last), weight in zip(CHUNKS, weights):
        out = product(spot, tokens, weight, BRIEF)
        out = out.reshape((-1,) + out.shape[2:])
        part = lax.all_to_all(out, ("c", "x"), 0, 0, tiled=True)
        preactivations = assemble(part, preactivations, first, last)
    anchor_new = anchor_new.transpose(1, 0, 2)
    momentum_new = momentum_new.transpose(1, 0, 2)
    return (preactivations, anchor_new, momentum_new)


def solution(mesh):
    fine = Mesh(mesh.devices.reshape(2, 4, 4, 4, 2), GROUP + ROWS)
    shard = P(GROUP, ROWS, None)
    in_specs = (
        shard,
        shard,
        shard,
        shard,
        P(ROWS, None, None),
        P(ROWS, None, GROUP),
        P(GROUP + ROWS, None),
    )
    out_specs = (P(GROUP + ROWS, None), P(ROWS, None, GROUP), P(ROWS, None, GROUP))
    return jax.shard_map(body, mesh=fine, in_specs=in_specs, out_specs=out_specs, check_vma=False)
```

time: 336 us -> 208 us (0.62)
  waiting for transfers between devices: 279 us -> 75.7 us
  starting transfers between devices: 0.12 us -> 54.1 us
  Pallas kernels: 0 us -> 32.9 us
  blocking collectives: 0 us -> 30.5 us
  matrix products: 14.3 us -> 0 us
  between operations: 13.8 us -> 0.73 us
  other arithmetic: 15.7 us -> 6.07 us
  local copies, waits for them, and re-layouts: 13.2 us -> 6.57 us
    all_gather x2 -> x0, waiting for transfers between devices: 235 us -> none  [the longest x1 187 us: body(): lax.all_gather(mixed_matrix, 'fsdp', axis=0, tiled=True)]
    ppermute x0 -> x13, waiting for transfers between devices: none -> 61.7 us  [shift(): return lax.ppermute(array, axis, [(i, (i + k) % n) for i in range(n)])]
    reduce_scatter x1 -> x0, waiting for transfers between devices: 43.9 us -> none  [body(): summed = lax.psum_scatter(pseudo, 'group', scatter_dimension=2, tiled=True)]
    pallas_call x0 -> x6, Pallas kernels: none -> 32.9 us  [the longest x2 13.8 us: product(): pl.pallas_call(product_kernel, grid_spec=pltpu.PrefetchScalarGridSpec(num...]
    all_to_all x0 -> x2, blocking collectives: none -> 30.5 us  [the longest x1 15.9 us: body(): part = lax.all_to_all(part, GROUP, 0, 0, tiled=True)]
    ppermute x0 -> x13, starting transfers between devices: none -> 27.8 us  [shift(): return lax.ppermute(array, axis, [(i, (i + k) % n) for i in range(n)])]
    all_to_all x0 -> x5, starting transfers between devices: none -> 26.3 us  [the longest x2 11.5 us: body(): part = lax.all_to_all(out, ('c', 'x'), 0, 0, tiled=True)]
    dot_general x1 -> x0, matrix products: 14.3 us -> none  [body(): jnp.dot(next_tokens, lax.all_gather(mixed_matrix, 'fsdp', axis=0, tiled=T...]
  transfers between devices with their start and end apart: 3 -> 18, of which waited for: 3 -> 9; matrix products, arithmetic and copies ran while one was open for 0% -> 5% of each run, Pallas kernels for 0% -> 14%
where the time goes in v1:
time: 208 us; the launch traced here: 207 us
  waiting for transfers between devices  75.7 us (36%)
  starting transfers between devices  54.1 us (26%)
  Pallas kernels  32.9 us (16%)
  blocking collectives  30.5 us (15%)
  local copies, waits for them, and re-layouts  6.57 us (3%)
  other arithmetic  6.07 us (3%)
    ppermute x13, waiting for transfers between devices, shift(): return lax.ppermute(array, axis, [(i, (i + k) % n) for i in range(n)])  61.7 us
    ppermute x13, starting transfers between devices, shift(): return lax.ppermute(array, axis, [(i, (i + k) % n) for i in range(n)])  27.8 us
    all_to_all x1, blocking collectives, body(): part = lax.all_to_all(part, GROUP, 0, 0, tiled=True)  15.9 us
    all_to_all x1, blocking collectives, body(): part = lax.all_to_all(after(part, held), PLANE, 0, 0, tiled=True)  14.6 us
    pallas_call x2, Pallas kernels, product(): pl.pallas_call(product_kernel, grid_spec=pltpu.PrefetchScalarGridSpec(num...  13.8 us
    all_to_all x2, waiting for transfers between devices, body(): part = lax.all_to_all(out, ('c', 'x'), 0, 0, tiled=True)  12.7 us
    all_to_all x2, starting transfers between devices, body(): part = lax.all_to_all(out, ('c', 'x'), 0, 0, tiled=True)  11.5 us
    pallas_call x1, Pallas kernels, inner_step(): pl.pallas_call(inner_kernel, grid=(SLICES,), in_specs=[wide] * 4 + [pl.Bl...  7.01 us
  transfers between devices with their start and end apart: 18, of which 9 were waited for; matrix products, arithmetic and copies ran while one was open for 5% of the time, Pallas kernels for 14%

profile of v1, /device:TPU:1, one launch (start us, length us, event | category | flops | bytes accessed | tf_op | source)
XLA Modules:
  0.0 206.6 jit_solution(738572248760598256)
XLA Ops:
  0.6 2.1 %collective-permute-start = (bf16[192,2048]{1,0:T(8,128)(2,1)}, bf16[192,2048]{1,0:T(8,128)(2,1)S(1)}, u32[]{:S(2)}, u32[]{:S(2)}) collective-permute-start(bf16[192,2048]{1,0:T(8,128)(2,1)} %param.13), channel_id=1, source_target_pairs={{0,2},{2,4},{4,6},{6,0},{1,3},{3,5},{5,7},{7,1},{8,10},{10,12},{12... | collective-permute-start | bytes 2359304 | tf_op jit(solution)/shard_map/ppermute | solution.py:167
  2.7 1.4 collective-permute-start.1
  4.1 7.0 %shard_map.94 = bf16[8,64,896]{2,1,0:T(8,128)(2,1)} custom-call(f32[64,7168]{1,0:T(8,128)} %bitcast.30, bf16[64,7168]{1,0:T(8,128)(2,1)} %bitcast.33, f32[64,7168]{1,0:T(8,128)} %bitcast.31, f32[64,7168]{1,0:T(8,128)} %bitcast.32, f32[7,64,1024]{2,1,0:T(8,128)} %bitcast.28), custom_call_target="tpu_custom_call" | custom-call | flops 1 | bytes 1 | tf_op jit(solution)/shard_map/pallas_call | solution.py:49
  11.1 5.7 %all-to-all-start = ((bf16[8,64,896]{2,1,0:T(8,128)(2,1)}), bf16[8,64,896]{2,1,0:T(8,128)(2,1)S(1)}, u32[]{:S(2)}, u32[]{:S(2)}) async-start(bf16[8,64,896]{2,1,0:T(8,128)(2,1)} %shard_map.94), calls=%async_computation | async-start | bytes 1835008 | tf_op jit(solution)/shard_map/all_to_all | solution.py:200
  16.8 0.9 constant_dynamic-update-slice_fusion.4
  17.7 1.5 collective-permute-done
  19.2 2.0 collective-permute-start.2
  21.2 0.0 collective-permute-done.1
  21.2 1.7 collective-permute-start.3
  22.9 0.9 constant_dynamic-update-slice_fusion.3
  23.8 0.9 constant_dynamic-update-slice_fusion.2
  24.8 4.4 %collective-permute-done.2 = bf16[96,2048]{1,0:T(8,128)(2,1)S(1)} collective-permute-done((bf16[96,2048]{1,0:T(8,128)(2,1)S(1)}, bf16[96,2048]{1,0:T(8,128)(2,1)S(1)}, u32[]{:S(2)}, u32[]{:S(2)}) %collective-permute-start.2) | collective-permute-done | bytes 393248 | tf_op jit(solution)/shard_map/ppermute | solution.py:167
  29.1 0.8 constant_dynamic-update-slice_fusion.1
  29.9 0.0 collective-permute-done.3
  29.9 0.8 constant_dynamic-update-slice_fusion
  30.7 3.7 %collective-permute-start.4 = (bf16[768,2048]{1,0:T(8,128)(2,1)}, bf16[768,2048]{1,0:T(8,128)(2,1)}, u32[]{:S(2)}, u32[]{:S(2)}) collective-permute-start(bf16[768,2048]{1,0:T(8,128)(2,1)} %constant_dynamic-update-slice_fusion), channel_id=1, source_target_pairs={{0,1},{1,0},{2,3},{3,2},{4,5},{5,4},{6,7},{7,6},{8,9},{9,8},{10,11... | collective-permute-start | bytes 9437192 | tf_op jit(solution)/shard_map/ppermute | solution.py:167
  34.4 0.0 all-to-all-done.pieces
  34.4 0.9 copy-done.2
  35.3 5.1 %shard_map.95 = (f32[7,64,128]{2,1,0:T(8,128)}, f32[7,64,128]{2,1,0:T(8,128)}, bf16[8,64,512]{2,1,0:T(8,128)(2,1)}, bf16[8,64,384]{2,1,0:T(8,128)(2,1)}) custom-call(s32[1]{0:T(128)} %bitcast.9.place, bf16[8,64,896]{2,1,0:T(8,128)(2,1)} %copy-done.2, f32[7,64,1024]{2,1,0:T(8,128)} %bitcast.29, f32[7,64,128]{2,1,0:T(8,128)} %bitcast.34), custom_call_target="tpu_custom_call" | custom-call | flops 1 | bytes 1 | tf_op jit(solution)/shard_map/pallas_call | solution.py:89
  40.4 15.9 %all_to_all.35 = bf16[8,64,512]{2,1,0:T(8,128)(2,1)S(1)} all-to-all(bf16[8,64,512]{2,1,0:T(8,128)(2,1)} %get-tuple-element.12), channel_id=1, replica_groups=mesh['zl'=2,'y'=4,'zh'=4,'x'=4,'c'=2] {'zl','y'}, dimensions={0} | all-to-all | bytes 1048576 | tf_op jit(solution)/shard_map/all_to_all | solution.py:207
  56.3 14.6 %all_to_all.36 = bf16[8,64,512]{2,1,0:T(8,128)(2,1)S(1)} all-to-all(bf16[8,64,512]{2,1,0:T(8,128)(2,1)S(1)} %all_to_all.35), channel_id=1, replica_groups=mesh['zl'=2,'y'=4,'zh'=4,'x'=4,'c'=2] {'x','c'}, dimensions={0} | all-to-all | bytes 1048576 | tf_op jit(solution)/shard_map/all_to_all | solution.py:208
  70.9 4.1 %all-to-all-start.1 = ((bf16[8,64,384]{2,1,0:T(8,128)(2,1)}), bf16[8,64,384]{2,1,0:T(8,128)(2,1)}, u32[]{:S(2)}, u32[]{:S(2)}) async-start(bf16[8,64,384]{2,1,0:T(8,128)(2,1)} %get-tuple-element.11), calls=%async_computation.1 | async-start | bytes 786432 | tf_op jit(solution)/shard_map/all_to_all | solution.py:207
  75.0 3.1 %collective-permute-start.5 = (bf16[512,512]{1,0:T(8,128)(2,1)S(1)}, bf16[512,512]{1,0:T(8,128)(2,1)S(1)}, u32[]{:S(2)}, u32[]{:S(2)}) collective-permute-start(bf16[512,512]{1,0:T(8,128)(2,1)S(1)} %bitcast.22), channel_id=1, source_target_pairs={{0,8},{8,16},{16,24},{24,0},{1,9},{9,17},{17,25},{25,1},{2,10},{10... | collective-permute-start | bytes 1572872 | tf_op jit(solution)/shard_map/ppermute | solution.py:167
  78.1 2.2 %collective-permute-start.6 = (bf16[512,512]{1,0:T(8,128)(2,1)S(1)}, bf16[512,512]{1,0:T(8,128)(2,1)S(1)}, u32[]{:S(2)}, u32[]{:S(2)}) collective-permute-start(bf16[512,512]{1,0:T(8,128)(2,1)S(1)} %bitcast.23), channel_id=1, source_target_pairs={{0,24},{8,0},{16,8},{24,16},{1,25},{9,1},{17,9},{25,17},{2,26},{10... | collective-permute-start | bytes 1572872 | tf_op jit(solution)/shard_map/ppermute | solution.py:167
  80.3 0.1 stack.40.place
  80.4 1.3 all-to-all-done.1
  81.7 25.2 %collective-permute-done.5.refs_1_ = bf16[512,512]{1,0:T(8,128)(2,1)S(1)} collective-permute-done((bf16[512,512]{1,0:T(8,128)(2,1)S(1)}, bf16[512,512]{1,0:T(8,128)(2,1)S(1)}, u32[]{:S(2)}, u32[]{:S(2)}) %collective-permute-start.5) | collective-permute-done | bytes 524320 | tf_op jit(solution)/shard_map/ppermute | solution.py:167
  106.9 0.0 collective-permute-done.6.refs_2_
  106.9 5.0 %all-to-all-start.4 = ((bf16[8,64,384]{2,1,0:T(8,128)(2,1)}), bf16[8,64,384]{2,1,0:T(8,128)(2,1)S(1)}, u32[]{:S(2)}, u32[]{:S(2)}) async-start(bf16[8,64,384]{2,1,0:T(8,128)(2,1)} %all-to-all-done.1), calls=%async_computation.4 | async-start | bytes 786432 | tf_op jit(solution)/shard_map/all_to_all | solution.py:208
  111.9 0.1 collective-permute-start.11
  112.1 3.7 %collective-permute-start.12 = (bf16[256,512]{1,0:T(8,128)(2,1)S(1)}, bf16[256,512]{1,0:T(8,128)(2,1)S(1)}, u32[]{:S(2)}, u32[]{:S(2)}) collective-permute-start(bf16[256,512]{1,0:T(8,128)(2,1)S(1)} %slice.29), channel_id=1, source_target_pairs={{0,24},{8,0},{16,8},{24,16},{1,25},{9,1},{17,9},{25,17},{2,26},{10... | collective-permute-start | bytes 786440 | tf_op jit(solution)/shard_map/ppermute | solution.py:167
  115.7 6.1 %pad_maximum_fusion.tokens = bf16[2,768,2048]{2,1,0:T(8,128)(2,1)} fusion(bf16[1,768,2048]{2,1,0:T(8,128)(2,1)} %bitcast.8, bf16[1,768,2048]{2,1,0:T(8,128)(2,1)} %bitcast.7), kind=kLoop, calls=%fused_computation | loop fusion | flops 3145728 | bytes 12582912 | tf_op jit(solution)/shard_map/stack | solution.py:214
  121.8 2.4 %collective-permute-done.11.refs_3_ = bf16[256,512]{1,0:T(8,128)(2,1)S(1)} collective-permute-done((bf16[256,512]{1,0:T(8,128)(2,1)S(1)}, bf16[256,512]{1,0:T(8,128)(2,1)S(1)}, u32[]{:S(2)}, u32[]{:S(2)}) %collective-permute-start.11) | collective-permute-done | bytes 262176 | tf_op jit(solution)/shard_map/ppermute | solution.py:167
  124.2 2.2 %collective-permute-done.12.refs_4_ = bf16[256,512]{1,0:T(8,128)(2,1)S(1)} collective-permute-done((bf16[256,512]{1,0:T(8,128)(2,1)S(1)}, bf16[256,512]{1,0:T(8,128)(2,1)S(1)}, u32[]{:S(2)}, u32[]{:S(2)}) %collective-permute-start.12) | collective-permute-done | bytes 262176 | tf_op jit(solution)/shard_map/ppermute | solution.py:167
  126.4 6.9 %shard_map.97 = bf16[2,4,192,512]{3,2,1,0:T(8,128)(2,1)} custom-call(s32[7]{0:T(128)S(1)} %stack.40.place, bf16[2,768,2048]{2,1,0:T(8,128)(2,1)} %pad_maximum_fusion.tokens, bf16[512,512]{1,0:T(8,128)(2,1)S(1)} %bitcast.24, bf16[512,512]{1,0:T(8,128)(2,1)S(1)} %collective-permute-done.5.refs_1_, bf16[512,512]{1,0:T(8,128)(2,1)S(1)} %collective-permute-done.6.refs_2_, ...), custom_call_target="tpu_custom_call" | custom-call | flops 1 | bytes 1 | tf_op jit(solution)/shard_map/pallas_call | solution.py:124
  133.4 5.8 %all-to-all-start.6 = ((bf16[8,192,512]{2,1,0:T(8,128)(2,1)}), bf16[8,192,512]{2,1,0:T(8,128)(2,1)S(1)}, u32[]{:S(2)}, u32[]{:S(2)}) async-start(bf16[8,192,512]{2,1,0:T(8,128)(2,1)} %bitcast.19), calls=%async_computation.6 | async-start | bytes 3145728 | tf_op jit(solution)/shard_map/all_to_all | solution.py:219
  139.1 0.8 collective-permute-start.7
  139.9 3.5 %collective-permute-start.8 = (bf16[512,384]{1,0:T(8,128)(2,1)S(1)}, bf16[512,384]{1,0:T(8,128)(2,1)S(1)}, u32[]{:S(2)}, u32[]{:S(2)}) collective-permute-start(bf16[512,384]{1,0:T(8,128)(2,1)S(1)} %bitcast.26), channel_id=1, source_target_pairs={{0,24},{8,0},{16,8},{24,16},{1,25},{9,1},{17,9},{25,17},{2,26},{10... | collective-permute-start | bytes 1179656 | tf_op jit(solution)/shard_map/ppermute | solution.py:167
  143.5 17.9 %collective-permute-done.7.refs_1_ = bf16[512,384]{1,0:T(8,128)(2,1)S(1)} collective-permute-done((bf16[512,384]{1,0:T(8,128)(2,1)S(1)}, bf16[512,384]{1,0:T(8,128)(2,1)S(1)}, u32[]{:S(2)}, u32[]{:S(2)}) %collective-permute-start.7) | collective-permute-done | bytes 393248 | tf_op jit(solution)/shard_map/ppermute | solution.py:167
  161.4 0.1 collective-permute-start.9
  161.5 3.6 %collective-permute-start.10 = (bf16[256,384]{1,0:T(8,128)(2,1)S(1)}, bf16[256,384]{1,0:T(8,128)(2,1)S(1)}, u32[]{:S(2)}, u32[]{:S(2)}) collective-permute-start(bf16[256,384]{1,0:T(8,128)(2,1)S(1)} %slice.27), channel_id=1, source_target_pairs={{0,24},{8,0},{16,8},{24,16},{1,25},{9,1},{17,9},{25,17},{2,26},{10... | collective-permute-start | bytes 589832 | tf_op jit(solution)/shard_map/ppermute | solution.py:167
  165.2 8.1 %collective-permute-done.9.refs_3_ = bf16[256,384]{1,0:T(8,128)(2,1)S(1)} collective-permute-done((bf16[256,384]{1,0:T(8,128)(2,1)S(1)}, bf16[256,384]{1,0:T(8,128)(2,1)S(1)}, u32[]{:S(2)}, u32[]{:S(2)}) %collective-permute-start.9) | collective-permute-done | bytes 196640 | tf_op jit(solution)/shard_map/ppermute | solution.py:167
  173.2 6.9 %shard_map.96 = bf16[2,4,192,384]{3,2,1,0:T(8,128)(2,1)} custom-call(s32[7]{0:T(128)S(1)} %stack.40.place, bf16[2,768,2048]{2,1,0:T(8,128)(2,1)} %pad_maximum_fusion.tokens, bf16[512,384]{1,0:T(8,128)(2,1)S(1)} %bitcast.27, bf16[512,384]{1,0:T(8,128)(2,1)S(1)} %collective-permute-done.7.refs_1_, bf16[512,384]{1,0:T(8,128)(2,1)S(1)} %collective-permute-done.8.refs_2_, ...), custom_call_target="tpu_custom_call" | custom-call | flops 1 | bytes 1 | tf_op jit(solution)/shard_map/pallas_call | solution.py:124
  180.1 5.8 %all-to-all-start.5 = ((bf16[8,192,384]{2,1,0:T(8,128)(2,1)}), bf16[8,192,384]{2,1,0:T(8,128)(2,1)S(1)}, u32[]{:S(2)}, u32[]{:S(2)}) async-start(bf16[8,192,384]{2,1,0:T(8,128)(2,1)} %bitcast.18), calls=%async_computation.5 | async-start | bytes 2359296 | tf_op jit(solution)/shard_map/all_to_all | solution.py:219
  185.9 3.7 %shard_map.98.refs_0_ = bf16[192,7168]{1,0:T(8,128)(2,1)} custom-call(bf16[8,192,512]{2,1,0:T(8,128)(2,1)} %copy-done), custom_call_target="tpu_custom_call" | custom-call | flops 1 | bytes 1 | tf_op jit(solution)/shard_map/pallas_call | solution.py:153
  189.6 12.7 %all-to-all-done.5.part = bf16[8,192,384]{2,1,0:T(8,128)(2,1)S(1)} async-done(((bf16[8,192,384]{2,1,0:T(8,128)(2,1)}), bf16[8,192,384]{2,1,0:T(8,128)(2,1)S(1)}, u32[]{:S(2)}, u32[]{:S(2)}) %all-to-all-start.5) | async-done | bytes 1179680 | tf_op jit(solution)/shard_map/all_to_all | solution.py:219
  202.3 1.0 copy-done.1
  203.3 3.2 %shard_map.99 = bf16[192,7168]{1,0:T(8,128)(2,1)} custom-call(bf16[8,192,384]{2,1,0:T(8,128)(2,1)} %copy-done.1, bf16[192,7168]{1,0:T(8,128)(2,1)} %shard_map.98.refs_0_), custom_call_target="tpu_custom_call", output_to_operand_aliasing={{}: (1, {})} | custom-call | flops 1 | bytes 1 | tf_op jit(solution)/shard_map/pallas_call | solution.py:153
  (17 shorter events, 0.2 us)
Async XLA Ops:
  0.6 18.6 %collective-permute-start = (bf16[192,2048]{1,0:T(8,128)(2,1)}, bf16[192,2048]{1,0:T(8,128)(2,1)S(1)}, u32[]{:S(2)}, u32[]{:S(2)}) collective-permute-start(bf16[192,2048]{1,0:T(8,128)(2,1)} %param.13), channel_id=1, source_target_pairs={{0,2},{2,4},{4,6},{6,0},{1,3},{3,5},{5,7},{7,1},{8,10},{10,12},{12... | collective-permute-start | bytes 2359304 | tf_op jit(solution)/shard_map/ppermute | solution.py:167
  2.7 18.4 %collective-permute-start.1 = (bf16[192,2048]{1,0:T(8,128)(2,1)}, bf16[192,2048]{1,0:T(8,128)(2,1)S(1)}, u32[]{:S(2)}, u32[]{:S(2)}) collective-permute-start(bf16[192,2048]{1,0:T(8,128)(2,1)} %param.13), channel_id=1, source_target_pairs={{0,6},{2,0},{4,2},{6,4},{1,7},{3,1},{5,3},{7,5},{8,14},{10,8},{12,... | collective-permute-start | bytes 2359304 | tf_op jit(solution)/shard_map/ppermute | solution.py:167
  4.1 12.7 %copy-start.3 = (bf16[192,2048]{1,0:T(8,128)(2,1)S(1)}, bf16[192,2048]{1,0:T(8,128)(2,1)}, u32[]{:S(2)}) copy-start(bf16[192,2048]{1,0:T(8,128)(2,1)} %param.13) | copy-start | bytes 2359300
  11.1 23.3 %all-to-all-start = ((bf16[8,64,896]{2,1,0:T(8,128)(2,1)}), bf16[8,64,896]{2,1,0:T(8,128)(2,1)S(1)}, u32[]{:S(2)}, u32[]{:S(2)}) async-start(bf16[8,64,896]{2,1,0:T(8,128)(2,1)} %shard_map.94), calls=%async_computation | async-start | bytes 1835008 | tf_op jit(solution)/shard_map/all_to_all | solution.py:200
  19.2 9.9 %collective-permute-start.2 = (bf16[96,2048]{1,0:T(8,128)(2,1)S(1)}, bf16[96,2048]{1,0:T(8,128)(2,1)S(1)}, u32[]{:S(2)}, u32[]{:S(2)}) collective-permute-start(bf16[96,2048]{1,0:T(8,128)(2,1)S(1)} %slice.24), channel_id=1, source_target_pairs={{0,2},{2,4},{4,6},{6,0},{1,3},{3,5},{5,7},{7,1},{8,10},{10,12},{12... | collective-permute-start | bytes 1179656 | tf_op jit(solution)/shard_map/ppermute | solution.py:167
  21.2 8.7 %collective-permute-start.3 = (bf16[96,2048]{1,0:T(8,128)(2,1)S(1)}, bf16[96,2048]{1,0:T(8,128)(2,1)S(1)}, u32[]{:S(2)}, u32[]{:S(2)}) collective-permute-start(bf16[96,2048]{1,0:T(8,128)(2,1)S(1)} %slice.25), channel_id=1, source_target_pairs={{0,6},{2,0},{4,2},{6,4},{1,7},{3,1},{5,3},{7,5},{8,14},{10,8},{12,... | collective-permute-start | bytes 1179656 | tf_op jit(solution)/shard_map/ppermute | solution.py:167
  30.7 85.0 %collective-permute-start.4 = (bf16[768,2048]{1,0:T(8,128)(2,1)}, bf16[768,2048]{1,0:T(8,128)(2,1)}, u32[]{:S(2)}, u32[]{:S(2)}) collective-permute-start(bf16[768,2048]{1,0:T(8,128)(2,1)} %constant_dynamic-update-slice_fusion), channel_id=1, source_target_pairs={{0,1},{1,0},{2,3},{3,2},{4,5},{5,4},{6,7},{7,6},{8,9},{9,8},{10,11... | collective-permute-start | bytes 9437192 | tf_op jit(solution)/shard_map/ppermute | solution.py:167
  34.4 0.9 copy-start.2
  70.9 10.8 %all-to-all-start.1 = ((bf16[8,64,384]{2,1,0:T(8,128)(2,1)}), bf16[8,64,384]{2,1,0:T(8,128)(2,1)}, u32[]{:S(2)}, u32[]{:S(2)}) async-start(bf16[8,64,384]{2,1,0:T(8,128)(2,1)} %get-tuple-element.11), calls=%async_computation.1 | async-start | bytes 786432 | tf_op jit(solution)/shard_map/all_to_all | solution.py:207
  75.0 31.9 %collective-permute-start.5 = (bf16[512,512]{1,0:T(8,128)(2,1)S(1)}, bf16[512,512]{1,0:T(8,128)(2,1)S(1)}, u32[]{:S(2)}, u32[]{:S(2)}) collective-permute-start(bf16[512,512]{1,0:T(8,128)(2,1)S(1)} %bitcast.22), channel_id=1, source_target_pairs={{0,8},{8,16},{16,24},{24,0},{1,9},{9,17},{17,25},{25,1},{2,10},{10... | collective-permute-start | bytes 1572872 | tf_op jit(solution)/shard_map/ppermute | solution.py:167
  78.1 28.9 %collective-permute-start.6 = (bf16[512,512]{1,0:T(8,128)(2,1)S(1)}, bf16[512,512]{1,0:T(8,128)(2,1)S(1)}, u32[]{:S(2)}, u32[]{:S(2)}) collective-permute-start(bf16[512,512]{1,0:T(8,128)(2,1)S(1)} %bitcast.23), channel_id=1, source_target_pairs={{0,24},{8,0},{16,8},{24,16},{1,25},{9,1},{17,9},{25,17},{2,26},{10... | collective-permute-start | bytes 1572872 | tf_op jit(solution)/shard_map/ppermute | solution.py:167
  106.9 26.4 %all-to-all-start.4 = ((bf16[8,64,384]{2,1,0:T(8,128)(2,1)}), bf16[8,64,384]{2,1,0:T(8,128)(2,1)S(1)}, u32[]{:S(2)}, u32[]{:S(2)}) async-start(bf16[8,64,384]{2,1,0:T(8,128)(2,1)} %all-to-all-done.1), calls=%async_computation.4 | async-start | bytes 786432 | tf_op jit(solution)/shard_map/all_to_all | solution.py:208
  111.9 12.3 %collective-permute-start.11 = (bf16[256,512]{1,0:T(8,128)(2,1)S(1)}, bf16[256,512]{1,0:T(8,128)(2,1)S(1)}, u32[]{:S(2)}, u32[]{:S(2)}) collective-permute-start(bf16[256,512]{1,0:T(8,128)(2,1)S(1)} %slice.28), channel_id=1, source_target_pairs={{0,8},{8,16},{16,24},{24,0},{1,9},{9,17},{17,25},{25,1},{2,10},{10... | collective-permute-start | bytes 786440 | tf_op jit(solution)/shard_map/ppermute | solution.py:167
  112.1 14.4 %collective-permute-start.12 = (bf16[256,512]{1,0:T(8,128)(2,1)S(1)}, bf16[256,512]{1,0:T(8,128)(2,1)S(1)}, u32[]{:S(2)}, u32[]{:S(2)}) collective-permute-start(bf16[256,512]{1,0:T(8,128)(2,1)S(1)} %slice.29), channel_id=1, source_target_pairs={{0,24},{8,0},{16,8},{24,16},{1,25},{9,1},{17,9},{25,17},{2,26},{10... | collective-permute-start | bytes 786440 | tf_op jit(solution)/shard_map/ppermute | solution.py:167
  133.4 46.7 %all-to-all-start.6 = ((bf16[8,192,512]{2,1,0:T(8,128)(2,1)}), bf16[8,192,512]{2,1,0:T(8,128)(2,1)S(1)}, u32[]{:S(2)}, u32[]{:S(2)}) async-start(bf16[8,192,512]{2,1,0:T(8,128)(2,1)} %bitcast.19), calls=%async_computation.6 | async-start | bytes 3145728 | tf_op jit(solution)/shard_map/all_to_all | solution.py:219
  139.1 22.2 %collective-permute-start.7 = (bf16[512,384]{1,0:T(8,128)(2,1)S(1)}, bf16[512,384]{1,0:T(8,128)(2,1)S(1)}, u32[]{:S(2)}, u32[]{:S(2)}) collective-permute-start(bf16[512,384]{1,0:T(8,128)(2,1)S(1)} %bitcast.25), channel_id=1, source_target_pairs={{0,8},{8,16},{16,24},{24,0},{1,9},{9,17},{17,25},{25,1},{2,10},{10... | collective-permute-start | bytes 1179656 | tf_op jit(solution)/shard_map/ppermute | solution.py:167
  139.9 21.5 %collective-permute-start.8 = (bf16[512,384]{1,0:T(8,128)(2,1)S(1)}, bf16[512,384]{1,0:T(8,128)(2,1)S(1)}, u32[]{:S(2)}, u32[]{:S(2)}) collective-permute-start(bf16[512,384]{1,0:T(8,128)(2,1)S(1)} %bitcast.26), channel_id=1, source_target_pairs={{0,24},{8,0},{16,8},{24,16},{1,25},{9,1},{17,9},{25,17},{2,26},{10... | collective-permute-start | bytes 1179656 | tf_op jit(solution)/shard_map/ppermute | solution.py:167
  161.4 11.8 %collective-permute-start.9 = (bf16[256,384]{1,0:T(8,128)(2,1)S(1)}, bf16[256,384]{1,0:T(8,128)(2,1)S(1)}, u32[]{:S(2)}, u32[]{:S(2)}) collective-permute-start(bf16[256,384]{1,0:T(8,128)(2,1)S(1)} %slice.26), channel_id=1, source_target_pairs={{0,8},{8,16},{16,24},{24,0},{1,9},{9,17},{17,25},{25,1},{2,10},{10... | collective-permute-start | bytes 589832 | tf_op jit(solution)/shard_map/ppermute | solution.py:167
  161.5 11.7 %collective-permute-start.10 = (bf16[256,384]{1,0:T(8,128)(2,1)S(1)}, bf16[256,384]{1,0:T(8,128)(2,1)S(1)}, u32[]{:S(2)}, u32[]{:S(2)}) collective-permute-start(bf16[256,384]{1,0:T(8,128)(2,1)S(1)} %slice.27), channel_id=1, source_target_pairs={{0,24},{8,0},{16,8},{24,16},{1,25},{9,1},{17,9},{25,17},{2,26},{10... | collective-permute-start | bytes 589832 | tf_op jit(solution)/shard_map/ppermute | solution.py:167
  180.1 5.8 %copy-start = (bf16[8,192,512]{2,1,0:T(8,128)(2,1)}, bf16[8,192,512]{2,1,0:T(8,128)(2,1)S(1)}, u32[]{:S(2)}) copy-start(bf16[8,192,512]{2,1,0:T(8,128)(2,1)S(1)} %all-to-all-done.6.part) | copy-start | bytes 4718596
  180.1 22.2 %all-to-all-start.5 = ((bf16[8,192,384]{2,1,0:T(8,128)(2,1)}), bf16[8,192,384]{2,1,0:T(8,128)(2,1)S(1)}, u32[]{:S(2)}, u32[]{:S(2)}) async-start(bf16[8,192,384]{2,1,0:T(8,128)(2,1)} %bitcast.18), calls=%async_computation.5 | async-start | bytes 2359296 | tf_op jit(solution)/shard_map/all_to_all | solution.py:219
  202.3 1.0 copy-start.1

commit v2 on v0

v2 whole, which is shorter than its diff:
```python
import functools

import jax
import jax.numpy as jnp
from jax import lax
from jax.experimental import pallas as pl
from jax.experimental.pallas import tpu as pltpu
from jax.sharding import Mesh
from jax.sharding import PartitionSpec as P

INNER_STEPS = 100

first_decay = 0.9
second_decay = 0.95
inner_rate = 0.04
weight_decay = 0.1
epsilon = 1e-08
momentum_decay = 0.9
outer_rate = 0.7
mixing = 0.5

GROUP = ("zl", "y")
ROWS = ("zh", "x", "c")
PLANE = ("x", "c")
SLICES = 7
LANES = 128
CUT = 4
STRIP = 4
WHOLE = pl.BlockSpec(memory_space=pltpu.VMEM)
ANYWHERE = pl.BlockSpec(memory_space=pl.ANY)
LARGE = pltpu.CompilerParams(vmem_limit_bytes=59 * 1024 * 1024)
BRIEF = pl.CostEstimate(flops=1, bytes_accessed=1, transcendentals=0)


def pseudo_gradient(weights, gradient, moment_one, moment_two, anchor):
    gradient = gradient.astype(jnp.float32)
    correct_one = 1.0 - first_decay**INNER_STEPS
    correct_two = 1.0 - second_decay**INNER_STEPS
    scale = inner_rate / correct_one
    first_new = (scale * first_decay) * moment_one + (scale * (1.0 - first_decay)) * gradient
    second_new = (second_decay / correct_two) * moment_two
    second_new = second_new + ((1.0 - second_decay) / correct_two) * (gradient * gradient)
    root = second_new * lax.rsqrt(second_new)
    step = first_new / (root + epsilon)
    return (anchor - (1.0 - inner_rate * weight_decay) * weights) + step


def inner_kernel(place, weights, grads, moment_one, moment_two, anchor, *refs):
    pieces, anchor_part, *held, arrived = refs
    slices, _, width = anchor.shape

    def parts(s):
        lanes = pl.ds(s * width, width)
        sources = [r.at[:, lanes] for r in (weights, grads, moment_one, moment_two)]
        return [
            pltpu.make_async_copy(source, into.at[s], arrived.at[s, i])
            for i, (source, into) in enumerate(zip(sources + [anchor.at[s]], held))
        ]

    copies = [parts(s) for s in range(slices)]
    for copy in sum(copies, []):
        copy.start()
    mine = pl.ds(pl.multiple_of(place[0] * LANES, LANES), LANES)
    for s in range(slices):
        for copy in copies[s]:
            copy.wait()
        pseudo = pseudo_gradient(*[h[s] for h in held]).astype(jnp.bfloat16)
        for g in range(pieces.shape[0]):
            pieces[g, :, s * LANES : (s + 1) * LANES] = pseudo[:, g * LANES : (g + 1) * LANES]
        anchor_part[s] = held[4][s, :, mine]


def inner_step(place, weights, grads, moment_one, moment_two, anchor, groups):
    slices, rows, _ = anchor.shape
    wide = pltpu.VMEM(anchor.shape, jnp.float32)
    return pl.pallas_call(
        inner_kernel,
        in_specs=[pl.BlockSpec(memory_space=pltpu.SMEM)] + [ANYWHERE] * 5,
        out_specs=[WHOLE] * 2,
        out_shape=[
            jax.ShapeDtypeStruct((groups, rows, slices * LANES), jnp.bfloat16),
            jax.ShapeDtypeStruct((slices, rows, LANES), jnp.float32),
        ],
        scratch_shapes=[wide, pltpu.VMEM(anchor.shape, jnp.bfloat16), wide, wide, wide]
        + [pltpu.SemaphoreType.DMA((slices, 5))],
        compiler_params=LARGE,
        cost_estimate=BRIEF,
    )(place, weights, grads, moment_one, moment_two, anchor)


def outer_kernel(pieces, anchor, momentum, anchor_new, momentum_new, mixed):
    groups = pieces.shape[0]
    for s in range(anchor.shape[0]):
        lanes = slice(s * LANES, (s + 1) * LANES)
        old = anchor[s]
        pseudo = [pieces[g, :, lanes].astype(jnp.float32) for g in range(groups)]
        mean_delta = sum(pseudo[1:], pseudo[0]) / groups
        after = momentum_decay * momentum[s] + mean_delta
        moved = old - outer_rate * (mean_delta + momentum_decay * after)
        momentum_new[s] = after
        anchor_new[s] = moved
        for g in range(groups):
            inner_new = old - pseudo[g]
            mixed[g, :, lanes] = (mixing * inner_new + (1.0 - mixing) * moved).astype(jnp.bfloat16)


def outer_step(pieces, anchor_part, momentum):
    new = jax.ShapeDtypeStruct(anchor_part.shape, jnp.float32)
    return pl.pallas_call(
        outer_kernel,
        in_specs=[WHOLE] * 3,
        out_specs=[WHOLE] * 3,
        out_shape=[new, new, jax.ShapeDtypeStruct(pieces.shape, jnp.bfloat16)],
        compiler_params=LARGE,
        cost_estimate=BRIEF,
    )(pieces, anchor_part, momentum)


def product_kernel(place, tokens, *refs):
    *weights, out = refs
    depth = weights[0].shape[0]
    total = None
    for k, weight in enumerate(weights):
        columns = pl.ds(pl.multiple_of(place[k], depth), depth)
        term = jnp.dot(tokens[:, columns], weight[...], preferred_element_type=jnp.float32)
        total = term if total is None else total + term
    out[...] = total.astype(jnp.bfloat16).reshape(out.shape)


def product(place, tokens, weights, pieces):
    rows, depth = tokens.shape
    width = weights[0].shape[1]
    return pl.pallas_call(
        product_kernel,
        grid_spec=pltpu.PrefetchScalarGridSpec(
            num_scalar_prefetch=1,
            grid=(pieces // STRIP,),
            in_specs=[pl.BlockSpec((STRIP * rows // pieces, depth), lambda i, p: (i, 0))]
            + [WHOLE] * len(weights),
            out_specs=pl.BlockSpec((STRIP, rows // pieces, width), lambda i, p: (i, 0, 0)),
        ),
        out_shape=jax.ShapeDtypeStruct((pieces, rows // pieces, width), jnp.bfloat16),
        compiler_params=pltpu.CompilerParams(vmem_limit_bytes=55 * 1024 * 1024),
        cost_estimate=BRIEF,
    )(place, tokens, *weights)


def assemble_kernel(first, part, *refs):
    out, left = refs[-2:]
    count, _, width = part.shape
    sent = []
    for j in range(count):
        for s in range(width // LANES):
            column = (first + s) * count + j
            sent.append(
                pltpu.make_async_copy(
                    part.at[j, :, pl.ds(s * LANES, LANES)],
                    out.at[:, pl.ds(column * LANES, LANES)],
                    left.at[j, s],
                )
            )
    for copy in sent:
        copy.start()
    for copy in sent:
        copy.wait()


def assemble(part, whole, first):
    count, rows, width = part.shape
    held = [] if whole is None else [whole]
    return pl.pallas_call(
        functools.partial(assemble_kernel, first),
        in_specs=[WHOLE] + [ANYWHERE] * len(held),
        out_specs=ANYWHERE,
        out_shape=jax.ShapeDtypeStruct((rows, SLICES * count * LANES), jnp.bfloat16),
        scratch_shapes=[pltpu.SemaphoreType.DMA((count, width // LANES))],
        input_output_aliases={1: 0} if held else {},
        compiler_params=pltpu.CompilerParams(vmem_limit_bytes=16 * 1024 * 1024),
        cost_estimate=BRIEF,
    )(part, *held)


def ring(array, axis):
    n = lax.axis_size(axis)
    pairs = [(2 * i + c, 2 * ((i + 1 - 2 * c) % n) + c) for i in range(n) for c in (0, 1)]
    return lax.ppermute(array, (axis, "c"), pairs)


def rings(block):
    blocks = [block]
    for _ in range(lax.axis_size("zh") - 1):
        blocks.append(ring(blocks[-1], "zh"))
    return blocks


def after(array, *earlier):
    return lax.optimization_barrier((array, earlier))[0]


def body(
    inner_weights, inner_grads, first_moment, second_moment, anchor, outer_momentum, next_tokens
):
    groups = lax.axis_size(GROUP)
    place = lax.axis_index(GROUP).astype(jnp.int32).reshape(1)
    turn = 2 * lax.axis_index("c") - 1
    deep = next_tokens.shape[1] // lax.axis_size("zh")
    spot = [
        (lax.axis_index("zh") + turn * k) % lax.axis_size("zh") * deep + half
        for half in (0, deep // 2)
        for k in range(4)
    ]
    spot = jnp.stack(spot).astype(jnp.int32)
    anchor = anchor.transpose(1, 0, 2)
    momentum = outer_momentum.transpose(1, 0, 2)
    state = (inner_weights[0], inner_grads[0], first_moment[0], second_moment[0], anchor)

    pieces, anchor_part = inner_step(place, *state, groups)
    pieces = lax.all_to_all(pieces, GROUP, 0, 0, tiled=True)
    anchor_new, momentum_new, mixed = outer_step(pieces, anchor_part, momentum)
    tokens = lax.all_gather(next_tokens, PLANE, axis=0, tiled=True)
    mixed = lax.all_to_all(mixed, GROUP, 0, 0, tiled=True)
    mixed = lax.all_to_all(mixed, PLANE, 0, 0, tiled=True)
    block = mixed.reshape(-1, mixed.shape[2])
    half = block.shape[0] // 2
    low, high = block[:half], block[half:]
    cut = CUT * LANES
    low_a, high_a = rings(low[:, :cut]), rings(high[:, :cut])
    low_b, high_b = rings(after(low[:, cut:], low_a)), rings(after(high[:, cut:], high_a))
    out_a = product(spot, tokens, low_a + high_a, lax.axis_size(PLANE))
    out_a = after(out_a, low_b[1], high_b[1])
    part_a = lax.all_to_all(out_a, PLANE, 0, 0, tiled=True)
    out_b = product(spot, tokens, low_b + high_b, lax.axis_size(PLANE))
    part_b = lax.all_to_all(out_b, PLANE, 0, 0, tiled=True)
    preactivations = assemble(part_a, None, 0)
    preactivations = assemble(part_b, preactivations, CUT)
    return (preactivations, anchor_new.transpose(1, 0, 2), momentum_new.transpose(1, 0, 2))


def solution(mesh):
    fine = Mesh(mesh.devices.reshape(2, 4, 4, 4, 2), GROUP + ROWS)
    shard = P(GROUP, ROWS, None)
    in_specs = (
        shard,
        shard,
        shard,
        shard,
        P(ROWS, None, None),
        P(ROWS, None, GROUP),
        P(GROUP + ROWS, None),
    )
    out_specs = (P(GROUP + ROWS, None), P(ROWS, None, GROUP), P(ROWS, None, GROUP))
    return jax.shard_map(body, mesh=fine, in_specs=in_specs, out_specs=out_specs, check_vma=False)
```

time: 336 us -> 189 us (0.56)
  waiting for transfers between devices: 279 us -> 47.8 us
  blocking collectives: 0 us -> 56 us
  starting transfers between devices: 0.12 us -> 43.6 us
  Pallas kernels: 0 us -> 25.3 us
  other arithmetic: 15.7 us -> 0 us
  matrix products: 14.3 us -> 0 us
  local copies, waits for them, and re-layouts: 13.2 us -> 1.5 us
    all_gather x2 -> x1, waiting for transfers between devices: 235 us -> 0.01 us  [body(): tokens = lax.all_gather(next_tokens, PLANE, axis=0, tiled=True)]
    all_to_all x0 -> x3, blocking collectives: none -> 56 us  [the longest x1 21.8 us: body(): mixed = lax.all_to_all(mixed, PLANE, 0, 0, tiled=True)]
    reduce_scatter x1 -> x0, waiting for transfers between devices: 43.9 us -> none  [body(): summed = lax.psum_scatter(pseudo, 'group', scatter_dimension=2, tiled=True)]
    ppermute x0 -> x12, starting transfers between devices: none -> 34.4 us  [ring(): return lax.ppermute(array, (axis, 'c'), pairs)]
    ppermute x0 -> x12, waiting for transfers between devices: none -> 32 us  [ring(): return lax.ppermute(array, (axis, 'c'), pairs)]
    pallas_call x0 -> x6, Pallas kernels: none -> 25.3 us  [the longest x2 15.1 us: product(): pl.pallas_call(product_kernel, grid_spec=pltpu.PrefetchScalarGridSpec(num...]
    all_to_all x0 -> x2, waiting for transfers between devices: none -> 15.1 us  [the longest x1 15.1 us: body(): part_b = lax.all_to_all(out_b, PLANE, 0, 0, tiled=True)]
    dot_general x1 -> x0, matrix products: 14.3 us -> none  [body(): jnp.dot(next_tokens, lax.all_gather(mixed_matrix, 'fsdp', axis=0, tiled=T...]
  transfers between devices with their start and end apart: 3 -> 15, of which waited for: 3 -> 11; matrix products, arithmetic and copies ran while one was open for 0% -> 0% of each run, Pallas kernels for 0% -> 13%
where the time goes in v2:
time: 189 us; the launch traced here: 188 us
  blocking collectives  56 us (30%)
  waiting for transfers between devices  47.8 us (25%)
  starting transfers between devices  43.6 us (23%)
  Pallas kernels  25.3 us (13%)
  between operations  14.3 us (8%)
    ppermute x12, starting transfers between devices, ring(): return lax.ppermute(array, (axis, 'c'), pairs)  34.4 us
    ppermute x12, waiting for transfers between devices, ring(): return lax.ppermute(array, (axis, 'c'), pairs)  32 us
    all_to_all x1, blocking collectives, body(): mixed = lax.all_to_all(mixed, PLANE, 0, 0, tiled=True)  21.8 us
    all_to_all x1, blocking collectives, body(): pieces = lax.all_to_all(pieces, GROUP, 0, 0, tiled=True)  19.3 us
    all_to_all x1, waiting for transfers between devices, body(): part_b = lax.all_to_all(out_b, PLANE, 0, 0, tiled=True)  15.1 us
    pallas_call x2, Pallas kernels, product(): pl.pallas_call(product_kernel, grid_spec=pltpu.PrefetchScalarGridSpec(num...  15.1 us
    all_to_all x1, blocking collectives, body(): mixed = lax.all_to_all(mixed, GROUP, 0, 0, tiled=True)  14.9 us
    all_to_all x1, starting transfers between devices, body(): part_b = lax.all_to_all(out_b, PLANE, 0, 0, tiled=True)  4.99 us
  transfers between devices with their start and end apart: 15, of which 11 were waited for; matrix products, arithmetic and copies ran while one was open for 0% of the time, Pallas kernels for 13%

profile of v2, /device:TPU:1, one launch (start us, length us, event | category | flops | bytes accessed | tf_op | source)
XLA Modules:
  0.0 188.5 jit_solution(17925590139220978685)
XLA Ops:
  7.2 0.0 all-gather.2.cloned.1.call-start
  7.2 0.7 all-gather.2.cloned.1.call-update
  7.9 4.8 %shard_map.94 = (bf16[8,64,896]{2,1,0:T(8,128)(2,1)}, f32[7,64,128]{2,1,0:T(8,128)}) custom-call(s32[1]{0:T(128)} %bitcast.8.place, f32[64,7168]{1,0:T(8,128)} %bitcast.23, bf16[64,7168]{1,0:T(8,128)(2,1)} %bitcast.27, f32[64,7168]{1,0:T(8,128)} %bitcast.24, f32[64,7168]{1,0:T(8,128)} %bitcast.25, f32[7,64,1024]{2,1,0:T(8,128)} %bitcast.26), custom_call_target="tpu_custom_call" | custom-call | flops 1 | bytes 1 | tf_op jit(solution)/shard_map/pallas_call | solution.py:76
  12.7 19.3 %all_to_all.25.pieces = bf16[8,64,896]{2,1,0:T(8,128)(2,1)} all-to-all(bf16[8,64,896]{2,1,0:T(8,128)(2,1)} %get-tuple-element.11), channel_id=1, replica_groups=mesh['zl'=2,'y'=4,'zh'=4,'x'=4,'c'=2] {'zl','y'}, dimensions={0} | all-to-all | bytes 1835008 | tf_op jit(solution)/shard_map/all_to_all | solution.py:218
  32.0 2.8 %shard_map.95 = (f32[7,64,128]{2,1,0:T(8,128)}, f32[7,64,128]{2,1,0:T(8,128)}, bf16[8,64,896]{2,1,0:T(8,128)(2,1)}) custom-call(bf16[8,64,896]{2,1,0:T(8,128)(2,1)} %all_to_all.25.pieces, f32[7,64,128]{2,1,0:T(8,128)} %get-tuple-element.12.anchor, f32[7,64,128]{2,1,0:T(8,128)} %bitcast.28), custom_call_target="tpu_custom_call" | custom-call | flops 1 | bytes 1 | tf_op jit(solution)/shard_map/pallas_call | solution.py:109
  34.8 14.9 %all_to_all.26 = bf16[8,64,896]{2,1,0:T(8,128)(2,1)S(1)} all-to-all(bf16[8,64,896]{2,1,0:T(8,128)(2,1)} %get-tuple-element.13), channel_id=1, replica_groups=mesh['zl'=2,'y'=4,'zh'=4,'x'=4,'c'=2] {'zl','y'}, dimensions={0} | all-to-all | bytes 1835008 | tf_op jit(solution)/shard_map/all_to_all | solution.py:221
  49.7 21.8 %all_to_all.27 = bf16[8,64,896]{2,1,0:T(8,128)(2,1)S(1)} all-to-all(bf16[8,64,896]{2,1,0:T(8,128)(2,1)S(1)} %all_to_all.26), channel_id=1, replica_groups=mesh['zl'=2,'y'=4,'zh'=4,'x'=4,'c'=2] {'x','c'}, dimensions={0} | all-to-all | bytes 1835008 | tf_op jit(solution)/shard_map/all_to_all | solution.py:222
  71.5 0.1 fusion
  71.6 0.0 copy-start
  71.6 5.2 %collective-permute-start.6 = (bf16[256,512]{1,0:T(8,128)(2,1)S(1)}, bf16[256,512]{1,0:T(8,128)(2,1)S(1)}, u32[]{:S(2)}, u32[]{:S(2)}) collective-permute-start(bf16[256,512]{1,0:T(8,128)(2,1)S(1)} %slice.37.refs_4_), channel_id=1, source_target_pairs={{0,8},{1,25},{8,16},{9,1},{16,24},{17,9},{24,0},{25,17},{2,10},{3,... | collective-permute-start | bytes 786440 | tf_op jit(solution)/shard_map/ppermute | solution.py:186
  76.8 0.0 copy-start.1
  76.9 1.2 collective-permute-start
  78.1 6.3 %collective-permute-done.6.refs_5_ = bf16[256,512]{1,0:T(8,128)(2,1)S(1)} collective-permute-done((bf16[256,512]{1,0:T(8,128)(2,1)S(1)}, bf16[256,512]{1,0:T(8,128)(2,1)S(1)}, u32[]{:S(2)}, u32[]{:S(2)}) %collective-permute-start.6) | collective-permute-done | bytes 262176 | tf_op jit(solution)/shard_map/ppermute | solution.py:186
  84.4 3.1 %collective-permute-start.7 = (bf16[256,512]{1,0:T(8,128)(2,1)S(1)}, bf16[256,512]{1,0:T(8,128)(2,1)S(1)}, u32[]{:S(2)}, u32[]{:S(2)}) collective-permute-start(bf16[256,512]{1,0:T(8,128)(2,1)S(1)} %collective-permute-done.6.refs_5_), channel_id=1, source_target_pairs={{0,8},{1,25},{8,16},{9,1},{16,24},{17,9},{24,0},{25,17},{2,10},{3,... | collective-permute-start | bytes 786440 | tf_op jit(solution)/shard_map/ppermute | solution.py:186
  87.5 2.1 %collective-permute-done.refs_1_ = bf16[256,512]{1,0:T(8,128)(2,1)S(1)} collective-permute-done((bf16[256,512]{1,0:T(8,128)(2,1)S(1)}, bf16[256,512]{1,0:T(8,128)(2,1)S(1)}, u32[]{:S(2)}, u32[]{:S(2)}) %collective-permute-start) | collective-permute-done | bytes 262176 | tf_op jit(solution)/shard_map/ppermute | solution.py:186
  89.5 3.6 %collective-permute-start.1 = (bf16[256,512]{1,0:T(8,128)(2,1)S(1)}, bf16[256,512]{1,0:T(8,128)(2,1)S(1)}, u32[]{:S(2)}, u32[]{:S(2)}) collective-permute-start(bf16[256,512]{1,0:T(8,128)(2,1)S(1)} %collective-permute-done.refs_1_), channel_id=1, source_target_pairs={{0,8},{1,25},{8,16},{9,1},{16,24},{17,9},{24,0},{25,17},{2,10},{3,... | collective-permute-start | bytes 786440 | tf_op jit(solution)/shard_map/ppermute | solution.py:186
  93.2 2.2 %collective-permute-done.7.refs_6_ = bf16[256,512]{1,0:T(8,128)(2,1)S(1)} collective-permute-done((bf16[256,512]{1,0:T(8,128)(2,1)S(1)}, bf16[256,512]{1,0:T(8,128)(2,1)S(1)}, u32[]{:S(2)}, u32[]{:S(2)}) %collective-permute-start.7) | collective-permute-done | bytes 262176 | tf_op jit(solution)/shard_map/ppermute | solution.py:186
  95.4 3.4 %collective-permute-start.8 = (bf16[256,512]{1,0:T(8,128)(2,1)S(1)}, bf16[256,512]{1,0:T(8,128)(2,1)S(1)}, u32[]{:S(2)}, u32[]{:S(2)}) collective-permute-start(bf16[256,512]{1,0:T(8,128)(2,1)S(1)} %collective-permute-done.7.refs_6_), channel_id=1, source_target_pairs={{0,8},{1,25},{8,16},{9,1},{16,24},{17,9},{24,0},{25,17},{2,10},{3,... | collective-permute-start | bytes 786440 | tf_op jit(solution)/shard_map/ppermute | solution.py:186
  98.8 2.9 %collective-permute-done.1.refs_2_ = bf16[256,512]{1,0:T(8,128)(2,1)S(1)} collective-permute-done((bf16[256,512]{1,0:T(8,128)(2,1)S(1)}, bf16[256,512]{1,0:T(8,128)(2,1)S(1)}, u32[]{:S(2)}, u32[]{:S(2)}) %collective-permute-start.1) | collective-permute-done | bytes 262176 | tf_op jit(solution)/shard_map/ppermute | solution.py:186
  101.7 3.2 %collective-permute-start.2 = (bf16[256,512]{1,0:T(8,128)(2,1)S(1)}, bf16[256,512]{1,0:T(8,128)(2,1)S(1)}, u32[]{:S(2)}, u32[]{:S(2)}) collective-permute-start(bf16[256,512]{1,0:T(8,128)(2,1)S(1)} %collective-permute-done.1.refs_2_), channel_id=1, source_target_pairs={{0,8},{1,25},{8,16},{9,1},{16,24},{17,9},{24,0},{25,17},{2,10},{3,... | collective-permute-start | bytes 786440 | tf_op jit(solution)/shard_map/ppermute | solution.py:186
  104.9 0.0 copy-start.2
  104.9 1.5 collective-permute-done.8.refs_7_
  106.5 3.2 %collective-permute-start.9 = (bf16[256,384]{1,0:T(8,128)(2,1)S(1)}, bf16[256,384]{1,0:T(8,128)(2,1)S(1)}, u32[]{:S(2)}, u32[]{:S(2)}) collective-permute-start(bf16[256,384]{1,0:T(8,128)(2,1)S(1)} %slice.36.refs_4_), channel_id=1, source_target_pairs={{0,8},{1,25},{8,16},{9,1},{16,24},{17,9},{24,0},{25,17},{2,10},{3,... | collective-permute-start | bytes 589832 | tf_op jit(solution)/shard_map/ppermute | solution.py:186
  109.7 1.0 collective-permute-done.2.refs_3_
  110.7 3.9 %collective-permute-start.3 = (bf16[256,384]{1,0:T(8,128)(2,1)S(1)}, bf16[256,384]{1,0:T(8,128)(2,1)S(1)}, u32[]{:S(2)}, u32[]{:S(2)}) collective-permute-start(bf16[256,384]{1,0:T(8,128)(2,1)S(1)} %slice.33.refs_0_), channel_id=1, source_target_pairs={{0,8},{1,25},{8,16},{9,1},{16,24},{17,9},{24,0},{25,17},{2,10},{3,... | collective-permute-start | bytes 589832 | tf_op jit(solution)/shard_map/ppermute | solution.py:186
  114.6 0.6 stack.35.place
  115.2 0.0 copy-done
  115.3 0.0 copy-done.4
  115.3 7.6 %shard_map.97 = bf16[8,192,512]{2,1,0:T(8,128)(2,1)} custom-call(s32[8]{0:T(128)} %stack.35.place, bf16[1536,2048]{1,0:T(8,128)(2,1)} %all-gather.2.cloned.1.call-done.tokens, bf16[256,512]{1,0:T(8,128)(2,1)} %copy-done.1, bf16[256,512]{1,0:T(8,128)(2,1)} %copy-done.5, bf16[256,512]{1,0:T(8,128)(2,1)} %copy-done.7, bf16[256,512]{1,0:T(8,128)(2,1)} %copy-done.9, ...), custom_call_target="tpu_custom_call" | custom-call | flops 1 | bytes 1 | tf_op jit(solution)/shard_map/pallas_call | solution.py:133
  122.9 0.0 copy-done.3
  122.9 0.0 collective-permute-done.9.refs_5_
  123.0 0.0 collective-permute-done.3.refs_1_
  123.0 4.2 %all-to-all-start.4 = ((bf16[8,192,512]{2,1,0:T(8,128)(2,1)}), bf16[8,192,512]{2,1,0:T(8,128)(2,1)S(1)}, u32[]{:S(2)}, u32[]{:S(2)}) async-start(bf16[8,192,512]{2,1,0:T(8,128)(2,1)} %shard_map.97), calls=%async_computation.4 | async-start | bytes 3145728 | tf_op jit(solution)/shard_map/all_to_all | solution.py:231
  127.2 2.4 %collective-permute-start.10 = (bf16[256,384]{1,0:T(8,128)(2,1)S(1)}, bf16[256,384]{1,0:T(8,128)(2,1)S(1)}, u32[]{:S(2)}, u32[]{:S(2)}) collective-permute-start(bf16[256,384]{1,0:T(8,128)(2,1)S(1)} %collective-permute-done.9.refs_5_), channel_id=1, source_target_pairs={{0,8},{1,25},{8,16},{9,1},{16,24},{17,9},{24,0},{25,17},{2,10},{3,... | collective-permute-start | bytes 589832 | tf_op jit(solution)/shard_map/ppermute | solution.py:186
  129.6 1.7 collective-permute-start.4
  131.3 6.4 %collective-permute-done.10.refs_6_ = bf16[256,384]{1,0:T(8,128)(2,1)S(1)} collective-permute-done((bf16[256,384]{1,0:T(8,128)(2,1)S(1)}, bf16[256,384]{1,0:T(8,128)(2,1)S(1)}, u32[]{:S(2)}, u32[]{:S(2)}) %collective-permute-start.10) | collective-permute-done | bytes 196640 | tf_op jit(solution)/shard_map/ppermute | solution.py:186
  137.7 1.7 collective-permute-start.11
  139.5 0.4 collective-permute-done.4.refs_2_
  139.8 1.7 collective-permute-start.5
  141.6 5.6 %collective-permute-done.11.refs_7_ = bf16[256,384]{1,0:T(8,128)(2,1)S(1)} collective-permute-done((bf16[256,384]{1,0:T(8,128)(2,1)S(1)}, bf16[256,384]{1,0:T(8,128)(2,1)S(1)}, u32[]{:S(2)}, u32[]{:S(2)}) %collective-permute-start.11) | collective-permute-done | bytes 196640 | tf_op jit(solution)/shard_map/ppermute | solution.py:186
  147.1 3.6 %collective-permute-done.5.refs_3_ = bf16[256,384]{1,0:T(8,128)(2,1)S(1)} collective-permute-done((bf16[256,384]{1,0:T(8,128)(2,1)S(1)}, bf16[256,384]{1,0:T(8,128)(2,1)S(1)}, u32[]{:S(2)}, u32[]{:S(2)}) %collective-permute-start.5) | collective-permute-done | bytes 196640 | tf_op jit(solution)/shard_map/ppermute | solution.py:186
  150.8 0.7 copy-done.15
  151.5 7.4 %shard_map.96 = bf16[8,192,384]{2,1,0:T(8,128)(2,1)} custom-call(s32[8]{0:T(128)} %stack.35.place, bf16[1536,2048]{1,0:T(8,128)(2,1)} %all-gather.2.cloned.1.call-done.tokens, bf16[256,384]{1,0:T(8,128)(2,1)} %copy-done.2, bf16[256,384]{1,0:T(8,128)(2,1)} %copy-done.11, bf16[256,384]{1,0:T(8,128)(2,1)} %copy-done.13, bf16[256,384]{1,0:T(8,128)(2,1)} %copy-done.15, ...), custom_call_target="tpu_custom_call" | custom-call | flops 1 | bytes 1 | tf_op jit(solution)/shard_map/pallas_call | solution.py:133
  158.9 0.0 all-to-all-done.4.part
  158.9 5.0 %all-to-all-start.3 = ((bf16[8,192,384]{2,1,0:T(8,128)(2,1)}), bf16[8,192,384]{2,1,0:T(8,128)(2,1)S(1)}, u32[]{:S(2)}, u32[]{:S(2)}) async-start(bf16[8,192,384]{2,1,0:T(8,128)(2,1)} %shard_map.96), calls=%async_computation.3 | async-start | bytes 2359296 | tf_op jit(solution)/shard_map/all_to_all | solution.py:233
  163.9 1.4 shard_map.98.refs_0_
  165.3 15.1 %all-to-all-done.3.part = bf16[8,192,384]{2,1,0:T(8,128)(2,1)S(1)} async-done(((bf16[8,192,384]{2,1,0:T(8,128)(2,1)}), bf16[8,192,384]{2,1,0:T(8,128)(2,1)S(1)}, u32[]{:S(2)}, u32[]{:S(2)}) %all-to-all-start.3) | async-done | bytes 1179680 | tf_op jit(solution)/shard_map/all_to_all | solution.py:233
  180.4 1.2 shard_map.99
  (30 shorter events, 0.1 us)
Async XLA Ops:
  7.2 108.1 %all-gather.2.cloned.1.call-start = ((), (), s32[]{:S(2)}) async-start(), calls=%async_computation.5 | async-start | bytes 7077888 | tf_op jit(solution)/shard_map/all_gather | solution.py:220
  71.6 43.7 %copy-start = (bf16[256,512]{1,0:T(8,128)(2,1)}, bf16[256,512]{1,0:T(8,128)(2,1)S(1)}, u32[]{:S(2)}) copy-start(bf16[256,512]{1,0:T(8,128)(2,1)S(1)} %slice.37.refs_4_) | copy-start | bytes 786436
  71.6 12.8 %collective-permute-start.6 = (bf16[256,512]{1,0:T(8,128)(2,1)S(1)}, bf16[256,512]{1,0:T(8,128)(2,1)S(1)}, u32[]{:S(2)}, u32[]{:S(2)}) collective-permute-start(bf16[256,512]{1,0:T(8,128)(2,1)S(1)} %slice.37.refs_4_), channel_id=1, source_target_pairs={{0,8},{1,25},{8,16},{9,1},{16,24},{17,9},{24,0},{25,17},{2,10},{3,... | collective-permute-start | bytes 786440 | tf_op jit(solution)/shard_map/ppermute | solution.py:186
  76.8 38.4 %copy-start.1 = (bf16[256,512]{1,0:T(8,128)(2,1)}, bf16[256,512]{1,0:T(8,128)(2,1)S(1)}, u32[]{:S(2)}) copy-start(bf16[256,512]{1,0:T(8,128)(2,1)S(1)} %slice.34.refs_0_) | copy-start | bytes 786436
  76.9 12.7 %collective-permute-start = (bf16[256,512]{1,0:T(8,128)(2,1)S(1)}, bf16[256,512]{1,0:T(8,128)(2,1)S(1)}, u32[]{:S(2)}, u32[]{:S(2)}) collective-permute-start(bf16[256,512]{1,0:T(8,128)(2,1)S(1)} %slice.34.refs_0_), channel_id=1, source_target_pairs={{0,8},{1,25},{8,16},{9,1},{16,24},{17,9},{24,0},{25,17},{2,10},{3,... | collective-permute-start | bytes 786440 | tf_op jit(solution)/shard_map/ppermute | solution.py:186
  84.4 30.9 %copy-start.4 = (bf16[256,512]{1,0:T(8,128)(2,1)}, bf16[256,512]{1,0:T(8,128)(2,1)S(1)}, u32[]{:S(2)}) copy-start(bf16[256,512]{1,0:T(8,128)(2,1)S(1)} %collective-permute-done.6.refs_5_) | copy-start | bytes 786436
  84.4 11.0 %collective-permute-start.7 = (bf16[256,512]{1,0:T(8,128)(2,1)S(1)}, bf16[256,512]{1,0:T(8,128)(2,1)S(1)}, u32[]{:S(2)}, u32[]{:S(2)}) collective-permute-start(bf16[256,512]{1,0:T(8,128)(2,1)S(1)} %collective-permute-done.6.refs_5_), channel_id=1, source_target_pairs={{0,8},{1,25},{8,16},{9,1},{16,24},{17,9},{24,0},{25,17},{2,10},{3,... | collective-permute-start | bytes 786440 | tf_op jit(solution)/shard_map/ppermute | solution.py:186
  89.5 25.7 %copy-start.5 = (bf16[256,512]{1,0:T(8,128)(2,1)}, bf16[256,512]{1,0:T(8,128)(2,1)S(1)}, u32[]{:S(2)}) copy-start(bf16[256,512]{1,0:T(8,128)(2,1)S(1)} %collective-permute-done.refs_1_) | copy-start | bytes 786436
  89.5 12.2 %collective-permute-start.1 = (bf16[256,512]{1,0:T(8,128)(2,1)S(1)}, bf16[256,512]{1,0:T(8,128)(2,1)S(1)}, u32[]{:S(2)}, u32[]{:S(2)}) collective-permute-start(bf16[256,512]{1,0:T(8,128)(2,1)S(1)} %collective-permute-done.refs_1_), channel_id=1, source_target_pairs={{0,8},{1,25},{8,16},{9,1},{16,24},{17,9},{24,0},{25,17},{2,10},{3,... | collective-permute-start | bytes 786440 | tf_op jit(solution)/shard_map/ppermute | solution.py:186
  95.4 19.9 %copy-start.6 = (bf16[256,512]{1,0:T(8,128)(2,1)}, bf16[256,512]{1,0:T(8,128)(2,1)S(1)}, u32[]{:S(2)}) copy-start(bf16[256,512]{1,0:T(8,128)(2,1)S(1)} %collective-permute-done.7.refs_6_) | copy-start | bytes 786436
  95.4 11.0 %collective-permute-start.8 = (bf16[256,512]{1,0:T(8,128)(2,1)S(1)}, bf16[256,512]{1,0:T(8,128)(2,1)S(1)}, u32[]{:S(2)}, u32[]{:S(2)}) collective-permute-start(bf16[256,512]{1,0:T(8,128)(2,1)S(1)} %collective-permute-done.7.refs_6_), channel_id=1, source_target_pairs={{0,8},{1,25},{8,16},{9,1},{16,24},{17,9},{24,0},{25,17},{2,10},{3,... | collective-permute-start | bytes 786440 | tf_op jit(solution)/shard_map/ppermute | solution.py:186
  101.7 13.6 %copy-start.7 = (bf16[256,512]{1,0:T(8,128)(2,1)}, bf16[256,512]{1,0:T(8,128)(2,1)S(1)}, u32[]{:S(2)}) copy-start(bf16[256,512]{1,0:T(8,128)(2,1)S(1)} %collective-permute-done.1.refs_2_) | copy-start | bytes 786436
  101.7 9.0 %collective-permute-start.2 = (bf16[256,512]{1,0:T(8,128)(2,1)S(1)}, bf16[256,512]{1,0:T(8,128)(2,1)S(1)}, u32[]{:S(2)}, u32[]{:S(2)}) collective-permute-start(bf16[256,512]{1,0:T(8,128)(2,1)S(1)} %collective-permute-done.1.refs_2_), channel_id=1, source_target_pairs={{0,8},{1,25},{8,16},{9,1},{16,24},{17,9},{24,0},{25,17},{2,10},{3,... | collective-permute-start | bytes 786440 | tf_op jit(solution)/shard_map/ppermute | solution.py:186
  104.9 18.0 %copy-start.2 = (bf16[256,384]{1,0:T(8,128)(2,1)}, bf16[256,384]{1,0:T(8,128)(2,1)S(1)}, u32[]{:S(2)}) copy-start(bf16[256,384]{1,0:T(8,128)(2,1)S(1)} %slice.33.refs_0_) | copy-start | bytes 589828
  104.9 18.0 %copy-start.3 = (bf16[256,384]{1,0:T(8,128)(2,1)}, bf16[256,384]{1,0:T(8,128)(2,1)S(1)}, u32[]{:S(2)}) copy-start(bf16[256,384]{1,0:T(8,128)(2,1)S(1)} %slice.36.refs_4_) | copy-start | bytes 589828
  106.4 8.8 %copy-start.8 = (bf16[256,512]{1,0:T(8,128)(2,1)}, bf16[256,512]{1,0:T(8,128)(2,1)S(1)}, u32[]{:S(2)}) copy-start(bf16[256,512]{1,0:T(8,128)(2,1)S(1)} %collective-permute-done.8.refs_7_) | copy-start | bytes 786436
  106.5 16.5 %collective-permute-start.9 = (bf16[256,384]{1,0:T(8,128)(2,1)S(1)}, bf16[256,384]{1,0:T(8,128)(2,1)S(1)}, u32[]{:S(2)}, u32[]{:S(2)}) collective-permute-start(bf16[256,384]{1,0:T(8,128)(2,1)S(1)} %slice.36.refs_4_), channel_id=1, source_target_pairs={{0,8},{1,25},{8,16},{9,1},{16,24},{17,9},{24,0},{25,17},{2,10},{3,... | collective-permute-start | bytes 589832 | tf_op jit(solution)/shard_map/ppermute | solution.py:186
  110.7 4.6 %copy-start.9 = (bf16[256,512]{1,0:T(8,128)(2,1)}, bf16[256,512]{1,0:T(8,128)(2,1)S(1)}, u32[]{:S(2)}) copy-start(bf16[256,512]{1,0:T(8,128)(2,1)S(1)} %collective-permute-done.2.refs_3_) | copy-start | bytes 786436
  110.7 12.3 %collective-permute-start.3 = (bf16[256,384]{1,0:T(8,128)(2,1)S(1)}, bf16[256,384]{1,0:T(8,128)(2,1)S(1)}, u32[]{:S(2)}, u32[]{:S(2)}) collective-permute-start(bf16[256,384]{1,0:T(8,128)(2,1)S(1)} %slice.33.refs_0_), channel_id=1, source_target_pairs={{0,8},{1,25},{8,16},{9,1},{16,24},{17,9},{24,0},{25,17},{2,10},{3,... | collective-permute-start | bytes 589832 | tf_op jit(solution)/shard_map/ppermute | solution.py:186
  123.0 27.8 %copy-start.10 = (bf16[256,384]{1,0:T(8,128)(2,1)}, bf16[256,384]{1,0:T(8,128)(2,1)S(1)}, u32[]{:S(2)}) copy-start(bf16[256,384]{1,0:T(8,128)(2,1)S(1)} %collective-permute-done.9.refs_5_) | copy-start | bytes 589828
  123.0 27.8 %copy-start.11 = (bf16[256,384]{1,0:T(8,128)(2,1)}, bf16[256,384]{1,0:T(8,128)(2,1)S(1)}, u32[]{:S(2)}) copy-start(bf16[256,384]{1,0:T(8,128)(2,1)S(1)} %collective-permute-done.3.refs_1_) | copy-start | bytes 589828
  123.0 35.9 %all-to-all-start.4 = ((bf16[8,192,512]{2,1,0:T(8,128)(2,1)}), bf16[8,192,512]{2,1,0:T(8,128)(2,1)S(1)}, u32[]{:S(2)}, u32[]{:S(2)}) async-start(bf16[8,192,512]{2,1,0:T(8,128)(2,1)} %shard_map.97), calls=%async_computation.4 | async-start | bytes 3145728 | tf_op jit(solution)/shard_map/all_to_all | solution.py:231
  127.2 10.5 %collective-permute-start.10 = (bf16[256,384]{1,0:T(8,128)(2,1)S(1)}, bf16[256,384]{1,0:T(8,128)(2,1)S(1)}, u32[]{:S(2)}, u32[]{:S(2)}) collective-permute-start(bf16[256,384]{1,0:T(8,128)(2,1)S(1)} %collective-permute-done.9.refs_5_), channel_id=1, source_target_pairs={{0,8},{1,25},{8,16},{9,1},{16,24},{17,9},{24,0},{25,17},{2,10},{3,... | collective-permute-start | bytes 589832 | tf_op jit(solution)/shard_map/ppermute | solution.py:186
  129.6 10.3 %collective-permute-start.4 = (bf16[256,384]{1,0:T(8,128)(2,1)S(1)}, bf16[256,384]{1,0:T(8,128)(2,1)S(1)}, u32[]{:S(2)}, u32[]{:S(2)}) collective-permute-start(bf16[256,384]{1,0:T(8,128)(2,1)S(1)} %collective-permute-done.3.refs_1_), channel_id=1, source_target_pairs={{0,8},{1,25},{8,16},{9,1},{16,24},{17,9},{24,0},{25,17},{2,10},{3,... | collective-permute-start | bytes 589832 | tf_op jit(solution)/shard_map/ppermute | solution.py:186
  137.7 13.0 %copy-start.12 = (bf16[256,384]{1,0:T(8,128)(2,1)}, bf16[256,384]{1,0:T(8,128)(2,1)S(1)}, u32[]{:S(2)}) copy-start(bf16[256,384]{1,0:T(8,128)(2,1)S(1)} %collective-permute-done.10.refs_6_) | copy-start | bytes 589828
  137.7 9.4 %collective-permute-start.11 = (bf16[256,384]{1,0:T(8,128)(2,1)S(1)}, bf16[256,384]{1,0:T(8,128)(2,1)S(1)}, u32[]{:S(2)}, u32[]{:S(2)}) collective-permute-start(bf16[256,384]{1,0:T(8,128)(2,1)S(1)} %collective-permute-done.10.refs_6_), channel_id=1, source_target_pairs={{0,8},{1,25},{8,16},{9,1},{16,24},{17,9},{24,0},{25,17},{2,10},{3,... | collective-permute-start | bytes 589832 | tf_op jit(solution)/shard_map/ppermute | solution.py:186
  139.8 10.9 %copy-start.13 = (bf16[256,384]{1,0:T(8,128)(2,1)}, bf16[256,384]{1,0:T(8,128)(2,1)S(1)}, u32[]{:S(2)}) copy-start(bf16[256,384]{1,0:T(8,128)(2,1)S(1)} %collective-permute-done.4.refs_2_) | copy-start | bytes 589828
  139.8 10.9 %collective-permute-start.5 = (bf16[256,384]{1,0:T(8,128)(2,1)S(1)}, bf16[256,384]{1,0:T(8,128)(2,1)S(1)}, u32[]{:S(2)}, u32[]{:S(2)}) collective-permute-start(bf16[256,384]{1,0:T(8,128)(2,1)S(1)} %collective-permute-done.4.refs_2_), channel_id=1, source_target_pairs={{0,8},{1,25},{8,16},{9,1},{16,24},{17,9},{24,0},{25,17},{2,10},{3,... | collective-permute-start | bytes 589832 | tf_op jit(solution)/shard_map/ppermute | solution.py:186
  147.1 3.6 %copy-start.14 = (bf16[256,384]{1,0:T(8,128)(2,1)}, bf16[256,384]{1,0:T(8,128)(2,1)S(1)}, u32[]{:S(2)}) copy-start(bf16[256,384]{1,0:T(8,128)(2,1)S(1)} %collective-permute-done.11.refs_7_) | copy-start | bytes 589828
  150.8 0.7 copy-start.15
  158.9 21.5 %all-to-all-start.3 = ((bf16[8,192,384]{2,1,0:T(8,128)(2,1)}), bf16[8,192,384]{2,1,0:T(8,128)(2,1)S(1)}, u32[]{:S(2)}, u32[]{:S(2)}) async-start(bf16[8,192,384]{2,1,0:T(8,128)(2,1)} %shard_map.96), calls=%async_computation.3 | async-start | bytes 2359296 | tf_op jit(solution)/shard_map/all_to_all | solution.py:233
Sparse Core Ops, SparseCore 0:
  9.8 47.6 all-gather.1

commit v3 on v2

--- a/solution.py
+++ b/solution.py
@@ -24,7 +24,7 @@
 PLANE = ("x", "c")
 SLICES = 7
 LANES = 128
-CUT = 4
+CUT = 5
 STRIP = 4
 WHOLE = pl.BlockSpec(memory_space=pltpu.VMEM)
 ANYWHERE = pl.BlockSpec(memory_space=pl.ANY)
@@ -225,7 +225,7 @@
     low, high = block[:half], block[half:]
     cut = CUT * LANES
     low_a, high_a = rings(low[:, :cut]), rings(high[:, :cut])
-    low_b, high_b = rings(after(low[:, cut:], low_a)), rings(after(high[:, cut:], high_a))
+    low_b, high_b = rings(after(low[:, cut:], low_a[:3])), rings(after(high[:, cut:], high_a[:3]))
     out_a = product(spot, tokens, low_a + high_a, lax.axis_size(PLANE))
     out_a = after(out_a, low_b[1], high_b[1])
     part_a = lax.all_to_all(out_a, PLANE, 0, 0, tiled=True)

time: 189 us -> 186 us (0.984)
  starting transfers between devices: 43.6 us -> 40.7 us
    all_to_all x1, waiting for transfers between devices: 15.1 us -> 10.7 us  [body(): part_b = lax.all_to_all(out_b, PLANE, 0, 0, tiled=True)]
    ppermute x12, starting transfers between devices: 34.4 us -> 32.3 us  [ring(): return lax.ppermute(array, (axis, 'c'), pairs)]
  transfers between devices with their start and end apart: 15 -> 15, of which waited for: 11 -> 10; matrix products, arithmetic and copies ran while one was open for 0% -> 0% of each run, Pallas kernels for 13% -> 13%
where the time goes in v3:
time: 186 us; the launch traced here: 185 us
  blocking collectives  56 us (30%)
  waiting for transfers between devices  46.8 us (25%)
  starting transfers between devices  40.7 us (22%)
  Pallas kernels  25.3 us (14%)
  between operations  14.3 us (8%)
  local copies, waits for them, and re-layouts  2.19 us (1%)
    ppermute x12, waiting for transfers between devices, ring(): return lax.ppermute(array, (axis, 'c'), pairs)  33.6 us
    ppermute x12, starting transfers between devices, ring(): return lax.ppermute(array, (axis, 'c'), pairs)  32.3 us
    all_to_all x1, blocking collectives, body(): mixed = lax.all_to_all(mixed, PLANE, 0, 0, tiled=True)  21.8 us
    all_to_all x1, blocking collectives, body(): pieces = lax.all_to_all(pieces, GROUP, 0, 0, tiled=True)  19.3 us
    pallas_call x2, Pallas kernels, product(): pl.pallas_call(product_kernel, grid_spec=pltpu.PrefetchScalarGridSpec(num...  15.2 us
    all_to_all x1, blocking collectives, body(): mixed = lax.all_to_all(mixed, GROUP, 0, 0, tiled=True)  14.9 us
    all_to_all x1, waiting for transfers between devices, body(): part_b = lax.all_to_all(out_b, PLANE, 0, 0, tiled=True)  10.7 us
    all_to_all x1, starting transfers between devices, body(): part_b = lax.all_to_all(out_b, PLANE, 0, 0, tiled=True)  4.82 us
  transfers between devices with their start and end apart: 15, of which 10 were waited for; matrix products, arithmetic and copies ran while one was open for 0% of the time, Pallas kernels for 13%

profile of v3, /device:TPU:1, one launch (start us, length us, event | category | flops | bytes accessed | tf_op | source)
XLA Modules:
  0.0 185.2 jit_solution(4899025191522523489)
XLA Ops:
  7.2 0.0 all-gather.2.cloned.1.call-start
  7.2 0.7 all-gather.2.cloned.1.call-update
  7.9 4.8 %shard_map.94 = (bf16[8,64,896]{2,1,0:T(8,128)(2,1)}, f32[7,64,128]{2,1,0:T(8,128)}) custom-call(s32[1]{0:T(128)} %bitcast.8.place, f32[64,7168]{1,0:T(8,128)} %bitcast.23, bf16[64,7168]{1,0:T(8,128)(2,1)} %bitcast.27, f32[64,7168]{1,0:T(8,128)} %bitcast.24, f32[64,7168]{1,0:T(8,128)} %bitcast.25, f32[7,64,1024]{2,1,0:T(8,128)} %bitcast.26), custom_call_target="tpu_custom_call" | custom-call | flops 1 | bytes 1 | tf_op jit(solution)/shard_map/pallas_call | solution.py:76
  12.7 19.3 %all_to_all.25.pieces = bf16[8,64,896]{2,1,0:T(8,128)(2,1)} all-to-all(bf16[8,64,896]{2,1,0:T(8,128)(2,1)} %get-tuple-element.11), channel_id=1, replica_groups=mesh['zl'=2,'y'=4,'zh'=4,'x'=4,'c'=2] {'zl','y'}, dimensions={0} | all-to-all | bytes 1835008 | tf_op jit(solution)/shard_map/all_to_all | solution.py:218
  32.0 2.8 %shard_map.95 = (f32[7,64,128]{2,1,0:T(8,128)}, f32[7,64,128]{2,1,0:T(8,128)}, bf16[8,64,896]{2,1,0:T(8,128)(2,1)}) custom-call(bf16[8,64,896]{2,1,0:T(8,128)(2,1)} %all_to_all.25.pieces, f32[7,64,128]{2,1,0:T(8,128)} %get-tuple-element.12.anchor, f32[7,64,128]{2,1,0:T(8,128)} %bitcast.28), custom_call_target="tpu_custom_call" | custom-call | flops 1 | bytes 1 | tf_op jit(solution)/shard_map/pallas_call | solution.py:109
  34.8 14.9 %all_to_all.26 = bf16[8,64,896]{2,1,0:T(8,128)(2,1)S(1)} all-to-all(bf16[8,64,896]{2,1,0:T(8,128)(2,1)} %get-tuple-element.13), channel_id=1, replica_groups=mesh['zl'=2,'y'=4,'zh'=4,'x'=4,'c'=2] {'zl','y'}, dimensions={0} | all-to-all | bytes 1835008 | tf_op jit(solution)/shard_map/all_to_all | solution.py:221
  49.7 21.8 %all_to_all.27 = bf16[8,64,896]{2,1,0:T(8,128)(2,1)S(1)} all-to-all(bf16[8,64,896]{2,1,0:T(8,128)(2,1)S(1)} %all_to_all.26), channel_id=1, replica_groups=mesh['zl'=2,'y'=4,'zh'=4,'x'=4,'c'=2] {'x','c'}, dimensions={0} | all-to-all | bytes 1835008 | tf_op jit(solution)/shard_map/all_to_all | solution.py:222
  71.5 0.1 fusion
  71.6 5.2 %collective-permute-start = (bf16[256,640]{1,0:T(8,128)(2,1)S(1)}, bf16[256,640]{1,0:T(8,128)(2,1)S(1)}, u32[]{:S(2)}, u32[]{:S(2)}) collective-permute-start(bf16[256,640]{1,0:T(8,128)(2,1)S(1)} %slice.34.refs_0_), channel_id=1, source_target_pairs={{0,8},{1,25},{8,16},{9,1},{16,24},{17,9},{24,0},{25,17},{2,10},{3,... | collective-permute-start | bytes 983048 | tf_op jit(solution)/shard_map/ppermute | solution.py:186
  76.9 1.2 collective-permute-start.5
  78.1 11.8 %collective-permute-done.refs_1_ = bf16[256,640]{1,0:T(8,128)(2,1)S(1)} collective-permute-done((bf16[256,640]{1,0:T(8,128)(2,1)S(1)}, bf16[256,640]{1,0:T(8,128)(2,1)S(1)}, u32[]{:S(2)}, u32[]{:S(2)}) %collective-permute-start) | collective-permute-done | bytes 327712 | tf_op jit(solution)/shard_map/ppermute | solution.py:186
  90.0 3.1 %collective-permute-start.1 = (bf16[256,640]{1,0:T(8,128)(2,1)S(1)}, bf16[256,640]{1,0:T(8,128)(2,1)S(1)}, u32[]{:S(2)}, u32[]{:S(2)}) collective-permute-start(bf16[256,640]{1,0:T(8,128)(2,1)S(1)} %collective-permute-done.refs_1_), channel_id=1, source_target_pairs={{0,8},{1,25},{8,16},{9,1},{16,24},{17,9},{24,0},{25,17},{2,10},{3,... | collective-permute-start | bytes 983048 | tf_op jit(solution)/shard_map/ppermute | solution.py:186
  93.0 7.2 %collective-permute-done.5.refs_5_ = bf16[256,640]{1,0:T(8,128)(2,1)S(1)} collective-permute-done((bf16[256,640]{1,0:T(8,128)(2,1)S(1)}, bf16[256,640]{1,0:T(8,128)(2,1)S(1)}, u32[]{:S(2)}, u32[]{:S(2)}) %collective-permute-start.5) | collective-permute-done | bytes 327712 | tf_op jit(solution)/shard_map/ppermute | solution.py:186
  100.2 3.1 %collective-permute-start.6 = (bf16[256,640]{1,0:T(8,128)(2,1)S(1)}, bf16[256,640]{1,0:T(8,128)(2,1)S(1)}, u32[]{:S(2)}, u32[]{:S(2)}) collective-permute-start(bf16[256,640]{1,0:T(8,128)(2,1)S(1)} %collective-permute-done.5.refs_5_), channel_id=1, source_target_pairs={{0,8},{1,25},{8,16},{9,1},{16,24},{17,9},{24,0},{25,17},{2,10},{3,... | collective-permute-start | bytes 983048 | tf_op jit(solution)/shard_map/ppermute | solution.py:186
  103.2 7.1 %collective-permute-done.1.refs_2_ = bf16[256,640]{1,0:T(8,128)(2,1)S(1)} collective-permute-done((bf16[256,640]{1,0:T(8,128)(2,1)S(1)}, bf16[256,640]{1,0:T(8,128)(2,1)S(1)}, u32[]{:S(2)}, u32[]{:S(2)}) %collective-permute-start.1) | collective-permute-done | bytes 327712 | tf_op jit(solution)/shard_map/ppermute | solution.py:186
  110.4 3.1 %collective-permute-start.10 = (bf16[256,640]{1,0:T(8,128)(2,1)S(1)}, bf16[256,640]{1,0:T(8,128)(2,1)S(1)}, u32[]{:S(2)}, u32[]{:S(2)}) collective-permute-start(bf16[256,640]{1,0:T(8,128)(2,1)S(1)} %collective-permute-done.1.refs_2_), channel_id=1, source_target_pairs={{0,8},{1,25},{8,16},{9,1},{16,24},{17,9},{24,0},{25,17},{2,10},{3,... | collective-permute-start | bytes 983048 | tf_op jit(solution)/shard_map/ppermute | solution.py:186
  113.5 0.4 collective-permute-done.6.refs_6_
  113.9 3.1 %collective-permute-start.11 = (bf16[256,640]{1,0:T(8,128)(2,1)S(1)}, bf16[256,640]{1,0:T(8,128)(2,1)S(1)}, u32[]{:S(2)}, u32[]{:S(2)}) collective-permute-start(bf16[256,640]{1,0:T(8,128)(2,1)S(1)} %collective-permute-done.6.refs_6_), channel_id=1, source_target_pairs={{0,8},{1,25},{8,16},{9,1},{16,24},{17,9},{24,0},{25,17},{2,10},{3,... | collective-permute-start | bytes 983048 | tf_op jit(solution)/shard_map/ppermute | solution.py:186
  117.0 0.0 copy-start.2
  117.0 0.0 copy-start.3
  117.0 2.3 %collective-permute-start.7 = (bf16[256,256]{1,0:T(8,128)(2,1)S(1)}, bf16[256,256]{1,0:T(8,128)(2,1)S(1)}, u32[]{:S(2)}, u32[]{:S(2)}) collective-permute-start(bf16[256,256]{1,0:T(8,128)(2,1)S(1)} %slice.36.refs_4_), channel_id=1, source_target_pairs={{0,8},{1,25},{8,16},{9,1},{16,24},{17,9},{24,0},{25,17},{2,10},{3,... | collective-permute-start | bytes 393224 | tf_op jit(solution)/shard_map/ppermute | solution.py:186
  119.4 1.5 collective-permute-start.2
  120.8 0.6 stack.35.place
  121.5 0.0 collective-permute-done.10.refs_3_
  121.5 0.5 collective-permute-done.11.refs_7_
  122.0 0.2 copy-done.8
  122.2 0.5 copy-done.9
  122.7 9.6 %shard_map.97 = bf16[8,192,640]{2,1,0:T(8,128)(2,1)} custom-call(s32[8]{0:T(128)} %stack.35.place, bf16[1536,2048]{1,0:T(8,128)(2,1)} %all-gather.2.cloned.1.call-done.tokens, bf16[256,640]{1,0:T(8,128)(2,1)} %copy-done, bf16[256,640]{1,0:T(8,128)(2,1)} %copy-done.4, bf16[256,640]{1,0:T(8,128)(2,1)} %copy-done.6, bf16[256,640]{1,0:T(8,128)(2,1)} %copy-done.8, ...), custom_call_target="tpu_custom_call" | custom-call | flops 1 | bytes 1 | tf_op jit(solution)/shard_map/pallas_call | solution.py:133
  132.2 0.0 copy-done.3
  132.2 0.0 collective-permute-done.7.refs_5_
  132.3 0.0 collective-permute-done.2.refs_1_
  132.3 3.6 %all-to-all-start.4 = ((bf16[8,192,640]{2,1,0:T(8,128)(2,1)}), bf16[8,192,640]{2,1,0:T(8,128)(2,1)S(1)}, u32[]{:S(2)}, u32[]{:S(2)}) async-start(bf16[8,192,640]{2,1,0:T(8,128)(2,1)} %shard_map.97), calls=%async_computation.4 | async-start | bytes 3932160 | tf_op jit(solution)/shard_map/all_to_all | solution.py:231
  135.9 3.4 %collective-permute-start.8 = (bf16[256,256]{1,0:T(8,128)(2,1)S(1)}, bf16[256,256]{1,0:T(8,128)(2,1)S(1)}, u32[]{:S(2)}, u32[]{:S(2)}) collective-permute-start(bf16[256,256]{1,0:T(8,128)(2,1)S(1)} %collective-permute-done.7.refs_5_), channel_id=1, source_target_pairs={{0,8},{1,25},{8,16},{9,1},{16,24},{17,9},{24,0},{25,17},{2,10},{3,... | collective-permute-start | bytes 393224 | tf_op jit(solution)/shard_map/ppermute | solution.py:186
  139.2 0.0 copy-done.11
  139.2 1.8 collective-permute-start.3
  141.0 2.5 %collective-permute-done.8.refs_6_ = bf16[256,256]{1,0:T(8,128)(2,1)S(1)} collective-permute-done((bf16[256,256]{1,0:T(8,128)(2,1)S(1)}, bf16[256,256]{1,0:T(8,128)(2,1)S(1)}, u32[]{:S(2)}, u32[]{:S(2)}) %collective-permute-start.8) | collective-permute-done | bytes 131104 | tf_op jit(solution)/shard_map/ppermute | solution.py:186
  143.5 2.0 %collective-permute-start.9 = (bf16[256,256]{1,0:T(8,128)(2,1)S(1)}, bf16[256,256]{1,0:T(8,128)(2,1)S(1)}, u32[]{:S(2)}, u32[]{:S(2)}) collective-permute-start(bf16[256,256]{1,0:T(8,128)(2,1)S(1)} %collective-permute-done.8.refs_6_), channel_id=1, source_target_pairs={{0,8},{1,25},{8,16},{9,1},{16,24},{17,9},{24,0},{25,17},{2,10},{3,... | collective-permute-start | bytes 393224 | tf_op jit(solution)/shard_map/ppermute | solution.py:186
  145.5 0.0 collective-permute-done.3.refs_2_
  145.5 2.6 %collective-permute-start.4 = (bf16[256,256]{1,0:T(8,128)(2,1)S(1)}, bf16[256,256]{1,0:T(8,128)(2,1)S(1)}, u32[]{:S(2)}, u32[]{:S(2)}) collective-permute-start(bf16[256,256]{1,0:T(8,128)(2,1)S(1)} %collective-permute-done.3.refs_2_), channel_id=1, source_target_pairs={{0,8},{1,25},{8,16},{9,1},{16,24},{17,9},{24,0},{25,17},{2,10},{3,... | collective-permute-start | bytes 393224 | tf_op jit(solution)/shard_map/ppermute | solution.py:186
  148.1 1.5 collective-permute-done.9.refs_7_
  149.6 2.7 %collective-permute-done.4.refs_3_ = bf16[256,256]{1,0:T(8,128)(2,1)S(1)} collective-permute-done((bf16[256,256]{1,0:T(8,128)(2,1)S(1)}, bf16[256,256]{1,0:T(8,128)(2,1)S(1)}, u32[]{:S(2)}, u32[]{:S(2)}) %collective-permute-start.4) | collective-permute-done | bytes 131104 | tf_op jit(solution)/shard_map/ppermute | solution.py:186
  152.3 0.6 copy-done.15
  152.9 5.6 %shard_map.96 = bf16[8,192,256]{2,1,0:T(8,128)(2,1)} custom-call(s32[8]{0:T(128)} %stack.35.place, bf16[1536,2048]{1,0:T(8,128)(2,1)} %all-gather.2.cloned.1.call-done.tokens, bf16[256,256]{1,0:T(8,128)(2,1)} %copy-done.3, bf16[256,256]{1,0:T(8,128)(2,1)} %copy-done.11, bf16[256,256]{1,0:T(8,128)(2,1)} %copy-done.13, bf16[256,256]{1,0:T(8,128)(2,1)} %copy-done.15, ...), custom_call_target="tpu_custom_call" | custom-call | flops 1 | bytes 1 | tf_op jit(solution)/shard_map/pallas_call | solution.py:133
  158.5 1.8 all-to-all-done.4.part
  160.3 4.8 %all-to-all-start.3 = ((bf16[8,192,256]{2,1,0:T(8,128)(2,1)}), bf16[8,192,256]{2,1,0:T(8,128)(2,1)S(1)}, u32[]{:S(2)}, u32[]{:S(2)}) async-start(bf16[8,192,256]{2,1,0:T(8,128)(2,1)} %shard_map.96), calls=%async_computation.3 | async-start | bytes 1572864 | tf_op jit(solution)/shard_map/all_to_all | solution.py:233
  165.1 1.6 shard_map.98.refs_0_
  166.7 10.7 %all-to-all-done.3.part = bf16[8,192,256]{2,1,0:T(8,128)(2,1)S(1)} async-done(((bf16[8,192,256]{2,1,0:T(8,128)(2,1)}), bf16[8,192,256]{2,1,0:T(8,128)(2,1)S(1)}, u32[]{:S(2)}, u32[]{:S(2)}) %all-to-all-start.3) | async-done | bytes 786464 | tf_op jit(solution)/shard_map/all_to_all | solution.py:233
  177.4 1.0 shard_map.99
  (30 shorter events, 0.1 us)
Async XLA Ops:
  7.2 114.8 %all-gather.2.cloned.1.call-start = ((), (), s32[]{:S(2)}) async-start(), calls=%async_computation.5 | async-start | bytes 7077888 | tf_op jit(solution)/shard_map/all_gather | solution.py:220
  71.6 50.3 %copy-start = (bf16[256,640]{1,0:T(8,128)(2,1)}, bf16[256,640]{1,0:T(8,128)(2,1)S(1)}, u32[]{:S(2)}) copy-start(bf16[256,640]{1,0:T(8,128)(2,1)S(1)} %slice.34.refs_0_) | copy-start | bytes 983044
  71.6 18.3 %collective-permute-start = (bf16[256,640]{1,0:T(8,128)(2,1)S(1)}, bf16[256,640]{1,0:T(8,128)(2,1)S(1)}, u32[]{:S(2)}, u32[]{:S(2)}) collective-permute-start(bf16[256,640]{1,0:T(8,128)(2,1)S(1)} %slice.34.refs_0_), channel_id=1, source_target_pairs={{0,8},{1,25},{8,16},{9,1},{16,24},{17,9},{24,0},{25,17},{2,10},{3,... | collective-permute-start | bytes 983048 | tf_op jit(solution)/shard_map/ppermute | solution.py:186
  76.9 45.1 %copy-start.1 = (bf16[256,640]{1,0:T(8,128)(2,1)}, bf16[256,640]{1,0:T(8,128)(2,1)S(1)}, u32[]{:S(2)}) copy-start(bf16[256,640]{1,0:T(8,128)(2,1)S(1)} %slice.37.refs_4_) | copy-start | bytes 983044
  76.9 23.3 %collective-permute-start.5 = (bf16[256,640]{1,0:T(8,128)(2,1)S(1)}, bf16[256,640]{1,0:T(8,128)(2,1)S(1)}, u32[]{:S(2)}, u32[]{:S(2)}) collective-permute-start(bf16[256,640]{1,0:T(8,128)(2,1)S(1)} %slice.37.refs_4_), channel_id=1, source_target_pairs={{0,8},{1,25},{8,16},{9,1},{16,24},{17,9},{24,0},{25,17},{2,10},{3,... | collective-permute-start | bytes 983048 | tf_op jit(solution)/shard_map/ppermute | solution.py:186
  90.0 32.0 %copy-start.4 = (bf16[256,640]{1,0:T(8,128)(2,1)}, bf16[256,640]{1,0:T(8,128)(2,1)S(1)}, u32[]{:S(2)}) copy-start(bf16[256,640]{1,0:T(8,128)(2,1)S(1)} %collective-permute-done.refs_1_) | copy-start | bytes 983044
  90.0 20.4 %collective-permute-start.1 = (bf16[256,640]{1,0:T(8,128)(2,1)S(1)}, bf16[256,640]{1,0:T(8,128)(2,1)S(1)}, u32[]{:S(2)}, u32[]{:S(2)}) collective-permute-start(bf16[256,640]{1,0:T(8,128)(2,1)S(1)} %collective-permute-done.refs_1_), channel_id=1, source_target_pairs={{0,8},{1,25},{8,16},{9,1},{16,24},{17,9},{24,0},{25,17},{2,10},{3,... | collective-permute-start | bytes 983048 | tf_op jit(solution)/shard_map/ppermute | solution.py:186
  100.2 21.8 %copy-start.5 = (bf16[256,640]{1,0:T(8,128)(2,1)}, bf16[256,640]{1,0:T(8,128)(2,1)S(1)}, u32[]{:S(2)}) copy-start(bf16[256,640]{1,0:T(8,128)(2,1)S(1)} %collective-permute-done.5.refs_5_) | copy-start | bytes 983044
  100.2 13.7 %collective-permute-start.6 = (bf16[256,640]{1,0:T(8,128)(2,1)S(1)}, bf16[256,640]{1,0:T(8,128)(2,1)S(1)}, u32[]{:S(2)}, u32[]{:S(2)}) collective-permute-start(bf16[256,640]{1,0:T(8,128)(2,1)S(1)} %collective-permute-done.5.refs_5_), channel_id=1, source_target_pairs={{0,8},{1,25},{8,16},{9,1},{16,24},{17,9},{24,0},{25,17},{2,10},{3,... | collective-permute-start | bytes 983048 | tf_op jit(solution)/shard_map/ppermute | solution.py:186
  110.4 11.6 %copy-start.6 = (bf16[256,640]{1,0:T(8,128)(2,1)}, bf16[256,640]{1,0:T(8,128)(2,1)S(1)}, u32[]{:S(2)}) copy-start(bf16[256,640]{1,0:T(8,128)(2,1)S(1)} %collective-permute-done.1.refs_2_) | copy-start | bytes 983044
  110.4 11.1 %collective-permute-start.10 = (bf16[256,640]{1,0:T(8,128)(2,1)S(1)}, bf16[256,640]{1,0:T(8,128)(2,1)S(1)}, u32[]{:S(2)}, u32[]{:S(2)}) collective-permute-start(bf16[256,640]{1,0:T(8,128)(2,1)S(1)} %collective-permute-done.1.refs_2_), channel_id=1, source_target_pairs={{0,8},{1,25},{8,16},{9,1},{16,24},{17,9},{24,0},{25,17},{2,10},{3,... | collective-permute-start | bytes 983048 | tf_op jit(solution)/shard_map/ppermute | solution.py:186
  113.9 8.1 %copy-start.7 = (bf16[256,640]{1,0:T(8,128)(2,1)}, bf16[256,640]{1,0:T(8,128)(2,1)S(1)}, u32[]{:S(2)}) copy-start(bf16[256,640]{1,0:T(8,128)(2,1)S(1)} %collective-permute-done.6.refs_6_) | copy-start | bytes 983044
  113.9 8.0 %collective-permute-start.11 = (bf16[256,640]{1,0:T(8,128)(2,1)S(1)}, bf16[256,640]{1,0:T(8,128)(2,1)S(1)}, u32[]{:S(2)}, u32[]{:S(2)}) collective-permute-start(bf16[256,640]{1,0:T(8,128)(2,1)S(1)} %collective-permute-done.6.refs_6_), channel_id=1, source_target_pairs={{0,8},{1,25},{8,16},{9,1},{16,24},{17,9},{24,0},{25,17},{2,10},{3,... | collective-permute-start | bytes 983048 | tf_op jit(solution)/shard_map/ppermute | solution.py:186
  117.0 15.2 %copy-start.2 = (bf16[256,256]{1,0:T(8,128)(2,1)}, bf16[256,256]{1,0:T(8,128)(2,1)S(1)}, u32[]{:S(2)}) copy-start(bf16[256,256]{1,0:T(8,128)(2,1)S(1)} %slice.36.refs_4_) | copy-start | bytes 393220
  117.0 15.2 %copy-start.3 = (bf16[256,256]{1,0:T(8,128)(2,1)}, bf16[256,256]{1,0:T(8,128)(2,1)S(1)}, u32[]{:S(2)}) copy-start(bf16[256,256]{1,0:T(8,128)(2,1)S(1)} %slice.33.refs_0_) | copy-start | bytes 393220
  117.0 15.2 %collective-permute-start.7 = (bf16[256,256]{1,0:T(8,128)(2,1)S(1)}, bf16[256,256]{1,0:T(8,128)(2,1)S(1)}, u32[]{:S(2)}, u32[]{:S(2)}) collective-permute-start(bf16[256,256]{1,0:T(8,128)(2,1)S(1)} %slice.36.refs_4_), channel_id=1, source_target_pairs={{0,8},{1,25},{8,16},{9,1},{16,24},{17,9},{24,0},{25,17},{2,10},{3,... | collective-permute-start | bytes 393224 | tf_op jit(solution)/shard_map/ppermute | solution.py:186
  119.4 12.9 %collective-permute-start.2 = (bf16[256,256]{1,0:T(8,128)(2,1)S(1)}, bf16[256,256]{1,0:T(8,128)(2,1)S(1)}, u32[]{:S(2)}, u32[]{:S(2)}) collective-permute-start(bf16[256,256]{1,0:T(8,128)(2,1)S(1)} %slice.33.refs_0_), channel_id=1, source_target_pairs={{0,8},{1,25},{8,16},{9,1},{16,24},{17,9},{24,0},{25,17},{2,10},{3,... | collective-permute-start | bytes 393224 | tf_op jit(solution)/shard_map/ppermute | solution.py:186
  121.5 0.8 copy-start.8
  121.9 0.8 copy-start.9
  132.2 3.6 %copy-start.10 = (bf16[256,256]{1,0:T(8,128)(2,1)}, bf16[256,256]{1,0:T(8,128)(2,1)S(1)}, u32[]{:S(2)}) copy-start(bf16[256,256]{1,0:T(8,128)(2,1)S(1)} %collective-permute-done.7.refs_5_) | copy-start | bytes 393220
  132.3 7.0 %copy-start.11 = (bf16[256,256]{1,0:T(8,128)(2,1)}, bf16[256,256]{1,0:T(8,128)(2,1)S(1)}, u32[]{:S(2)}) copy-start(bf16[256,256]{1,0:T(8,128)(2,1)S(1)} %collective-permute-done.2.refs_1_) | copy-start | bytes 393220
  132.3 28.0 %all-to-all-start.4 = ((bf16[8,192,640]{2,1,0:T(8,128)(2,1)}), bf16[8,192,640]{2,1,0:T(8,128)(2,1)S(1)}, u32[]{:S(2)}, u32[]{:S(2)}) async-start(bf16[8,192,640]{2,1,0:T(8,128)(2,1)} %shard_map.97), calls=%async_computation.4 | async-start | bytes 3932160 | tf_op jit(solution)/shard_map/all_to_all | solution.py:231
  135.9 7.6 %collective-permute-start.8 = (bf16[256,256]{1,0:T(8,128)(2,1)S(1)}, bf16[256,256]{1,0:T(8,128)(2,1)S(1)}, u32[]{:S(2)}, u32[]{:S(2)}) collective-permute-start(bf16[256,256]{1,0:T(8,128)(2,1)S(1)} %collective-permute-done.7.refs_5_), channel_id=1, source_target_pairs={{0,8},{1,25},{8,16},{9,1},{16,24},{17,9},{24,0},{25,17},{2,10},{3,... | collective-permute-start | bytes 393224 | tf_op jit(solution)/shard_map/ppermute | solution.py:186
  139.2 6.2 %collective-permute-start.3 = (bf16[256,256]{1,0:T(8,128)(2,1)S(1)}, bf16[256,256]{1,0:T(8,128)(2,1)S(1)}, u32[]{:S(2)}, u32[]{:S(2)}) collective-permute-start(bf16[256,256]{1,0:T(8,128)(2,1)S(1)} %collective-permute-done.2.refs_1_), channel_id=1, source_target_pairs={{0,8},{1,25},{8,16},{9,1},{16,24},{17,9},{24,0},{25,17},{2,10},{3,... | collective-permute-start | bytes 393224 | tf_op jit(solution)/shard_map/ppermute | solution.py:186
  143.5 8.8 %copy-start.12 = (bf16[256,256]{1,0:T(8,128)(2,1)}, bf16[256,256]{1,0:T(8,128)(2,1)S(1)}, u32[]{:S(2)}) copy-start(bf16[256,256]{1,0:T(8,128)(2,1)S(1)} %collective-permute-done.8.refs_6_) | copy-start | bytes 393220
  143.5 6.1 %collective-permute-start.9 = (bf16[256,256]{1,0:T(8,128)(2,1)S(1)}, bf16[256,256]{1,0:T(8,128)(2,1)S(1)}, u32[]{:S(2)}, u32[]{:S(2)}) collective-permute-start(bf16[256,256]{1,0:T(8,128)(2,1)S(1)} %collective-permute-done.8.refs_6_), channel_id=1, source_target_pairs={{0,8},{1,25},{8,16},{9,1},{16,24},{17,9},{24,0},{25,17},{2,10},{3,... | collective-permute-start | bytes 393224 | tf_op jit(solution)/shard_map/ppermute | solution.py:186
  145.5 6.8 %copy-start.13 = (bf16[256,256]{1,0:T(8,128)(2,1)}, bf16[256,256]{1,0:T(8,128)(2,1)S(1)}, u32[]{:S(2)}) copy-start(bf16[256,256]{1,0:T(8,128)(2,1)S(1)} %collective-permute-done.3.refs_2_) | copy-start | bytes 393220
  145.5 6.8 %collective-permute-start.4 = (bf16[256,256]{1,0:T(8,128)(2,1)S(1)}, bf16[256,256]{1,0:T(8,128)(2,1)S(1)}, u32[]{:S(2)}, u32[]{:S(2)}) collective-permute-start(bf16[256,256]{1,0:T(8,128)(2,1)S(1)} %collective-permute-done.3.refs_2_), channel_id=1, source_target_pairs={{0,8},{1,25},{8,16},{9,1},{16,24},{17,9},{24,0},{25,17},{2,10},{3,... | collective-permute-start | bytes 393224 | tf_op jit(solution)/shard_map/ppermute | solution.py:186
  149.6 2.7 %copy-start.14 = (bf16[256,256]{1,0:T(8,128)(2,1)}, bf16[256,256]{1,0:T(8,128)(2,1)S(1)}, u32[]{:S(2)}) copy-start(bf16[256,256]{1,0:T(8,128)(2,1)S(1)} %collective-permute-done.9.refs_7_) | copy-start | bytes 393220
  152.3 0.7 copy-start.15
  160.3 17.1 %all-to-all-start.3 = ((bf16[8,192,256]{2,1,0:T(8,128)(2,1)}), bf16[8,192,256]{2,1,0:T(8,128)(2,1)S(1)}, u32[]{:S(2)}, u32[]{:S(2)}) async-start(bf16[8,192,256]{2,1,0:T(8,128)(2,1)} %shard_map.96), calls=%async_computation.3 | async-start | bytes 1572864 | tf_op jit(solution)/shard_map/all_to_all | solution.py:233
Sparse Core Ops, SparseCore 0:
  9.8 47.6 all-gather.1

commit v4 on v3

--- a/solution.py
+++ b/solution.py
@@ -25,7 +25,6 @@
 SLICES = 7
 LANES = 128
 CUT = 5
-STRIP = 4
 WHOLE = pl.BlockSpec(memory_space=pltpu.VMEM)
 ANYWHERE = pl.BlockSpec(memory_space=pl.ANY)
 LARGE = pltpu.CompilerParams(vmem_limit_bytes=59 * 1024 * 1024)
@@ -127,17 +126,17 @@
     out[...] = total.astype(jnp.bfloat16).reshape(out.shape)
 
 
-def product(place, tokens, weights, pieces):
+def product(place, tokens, weights, pieces, strip):
     rows, depth = tokens.shape
     width = weights[0].shape[1]
     return pl.pallas_call(
         product_kernel,
         grid_spec=pltpu.PrefetchScalarGridSpec(
             num_scalar_prefetch=1,
-            grid=(pieces // STRIP,),
-            in_specs=[pl.BlockSpec((STRIP * rows // pieces, depth), lambda i, p: (i, 0))]
+            grid=(pieces // strip,),
+            in_specs=[pl.BlockSpec((strip * rows // pieces, depth), lambda i, p: (i, 0))]
             + [WHOLE] * len(weights),
-            out_specs=pl.BlockSpec((STRIP, rows // pieces, width), lambda i, p: (i, 0, 0)),
+            out_specs=pl.BlockSpec((strip, rows // pieces, width), lambda i, p: (i, 0, 0)),
         ),
         out_shape=jax.ShapeDtypeStruct((pieces, rows // pieces, width), jnp.bfloat16),
         compiler_params=pltpu.CompilerParams(vmem_limit_bytes=55 * 1024 * 1024),
@@ -226,10 +225,10 @@
     cut = CUT * LANES
     low_a, high_a = rings(low[:, :cut]), rings(high[:, :cut])
     low_b, high_b = rings(after(low[:, cut:], low_a[:3])), rings(after(high[:, cut:], high_a[:3]))
-    out_a = product(spot, tokens, low_a + high_a, lax.axis_size(PLANE))
+    out_a = product(spot, tokens, low_a + high_a, lax.axis_size(PLANE), 4)
     out_a = after(out_a, low_b[1], high_b[1])
     part_a = lax.all_to_all(out_a, PLANE, 0, 0, tiled=True)
-    out_b = product(spot, tokens, low_b + high_b, lax.axis_size(PLANE))
+    out_b = product(spot, tokens, low_b + high_b, lax.axis_size(PLANE), 2)
     part_b = lax.all_to_all(out_b, PLANE, 0, 0, tiled=True)
     preactivations = assemble(part_a, None, 0)
     preactivations = assemble(part_b, preactivations, CUT)

time: 186 us -> 187 us (level)
  transfers between devices with their start and end apart: 15 -> 15, of which waited for: 10 -> 10; matrix products, arithmetic and copies ran while one was open for 0% -> 0% of each run, Pallas kernels for 13% -> 14%
where the time goes in v4:
time: 187 us; the launch traced here: 186 us
  blocking collectives  56 us (30%)
  waiting for transfers between devices  46 us (25%)
  starting transfers between devices  41.5 us (22%)
  Pallas kernels  26.1 us (14%)
  between operations  14.3 us (8%)
  local copies, waits for them, and re-layouts  2.19 us (1%)
    ppermute x12, waiting for transfers between devices, ring(): return lax.ppermute(array, (axis, 'c'), pairs)  33.6 us
    ppermute x12, starting transfers between devices, ring(): return lax.ppermute(array, (axis, 'c'), pairs)  32.3 us
    all_to_all x1, blocking collectives, body(): mixed = lax.all_to_all(mixed, PLANE, 0, 0, tiled=True)  21.8 us
    all_to_all x1, blocking collectives, body(): pieces = lax.all_to_all(pieces, GROUP, 0, 0, tiled=True)  19.3 us
    pallas_call x2, Pallas kernels, product(): pl.pallas_call(product_kernel, grid_spec=pltpu.PrefetchScalarGridSpec(num...  16 us
    all_to_all x1, blocking collectives, body(): mixed = lax.all_to_all(mixed, GROUP, 0, 0, tiled=True)  14.9 us
    all_to_all x1, waiting for transfers between devices, body(): part_b = lax.all_to_all(out_b, PLANE, 0, 0, tiled=True)  10.7 us
    all_to_all x1, starting transfers between devices, body(): part_b = lax.all_to_all(out_b, PLANE, 0, 0, tiled=True)  5.62 us
  transfers between devices with their start and end apart: 15, of which 10 were waited for; matrix products, arithmetic and copies ran while one was open for 0% of the time, Pallas kernels for 14%

profile of v4, /device:TPU:1, one launch (start us, length us, event | category | flops | bytes accessed | tf_op | source)
XLA Modules:
  0.0 186.0 jit_solution(276602733696772854)
XLA Ops:
  7.2 0.0 all-gather.2.cloned.1.call-start
  7.2 0.7 all-gather.2.cloned.1.call-update
  7.9 4.8 %shard_map.94 = (bf16[8,64,896]{2,1,0:T(8,128)(2,1)}, f32[7,64,128]{2,1,0:T(8,128)}) custom-call(s32[1]{0:T(128)} %bitcast.8.place, f32[64,7168]{1,0:T(8,128)} %bitcast.23, bf16[64,7168]{1,0:T(8,128)(2,1)} %bitcast.27, f32[64,7168]{1,0:T(8,128)} %bitcast.24, f32[64,7168]{1,0:T(8,128)} %bitcast.25, f32[7,64,1024]{2,1,0:T(8,128)} %bitcast.26), custom_call_target="tpu_custom_call" | custom-call | flops 1 | bytes 1 | tf_op jit(solution)/shard_map/pallas_call | solution.py:75
  12.7 19.3 %all_to_all.25.pieces = bf16[8,64,896]{2,1,0:T(8,128)(2,1)} all-to-all(bf16[8,64,896]{2,1,0:T(8,128)(2,1)} %get-tuple-element.11), channel_id=1, replica_groups=mesh['zl'=2,'y'=4,'zh'=4,'x'=4,'c'=2] {'zl','y'}, dimensions={0} | all-to-all | bytes 1835008 | tf_op jit(solution)/shard_map/all_to_all | solution.py:217
  32.0 2.8 %shard_map.95 = (f32[7,64,128]{2,1,0:T(8,128)}, f32[7,64,128]{2,1,0:T(8,128)}, bf16[8,64,896]{2,1,0:T(8,128)(2,1)}) custom-call(bf16[8,64,896]{2,1,0:T(8,128)(2,1)} %all_to_all.25.pieces, f32[7,64,128]{2,1,0:T(8,128)} %get-tuple-element.12.anchor, f32[7,64,128]{2,1,0:T(8,128)} %bitcast.28), custom_call_target="tpu_custom_call" | custom-call | flops 1 | bytes 1 | tf_op jit(solution)/shard_map/pallas_call | solution.py:108
  34.8 14.9 %all_to_all.26 = bf16[8,64,896]{2,1,0:T(8,128)(2,1)S(1)} all-to-all(bf16[8,64,896]{2,1,0:T(8,128)(2,1)} %get-tuple-element.13), channel_id=1, replica_groups=mesh['zl'=2,'y'=4,'zh'=4,'x'=4,'c'=2] {'zl','y'}, dimensions={0} | all-to-all | bytes 1835008 | tf_op jit(solution)/shard_map/all_to_all | solution.py:220
  49.7 21.8 %all_to_all.27 = bf16[8,64,896]{2,1,0:T(8,128)(2,1)S(1)} all-to-all(bf16[8,64,896]{2,1,0:T(8,128)(2,1)S(1)} %all_to_all.26), channel_id=1, replica_groups=mesh['zl'=2,'y'=4,'zh'=4,'x'=4,'c'=2] {'x','c'}, dimensions={0} | all-to-all | bytes 1835008 | tf_op jit(solution)/shard_map/all_to_all | solution.py:221
  71.5 0.1 fusion
  71.6 5.2 %collective-permute-start = (bf16[256,640]{1,0:T(8,128)(2,1)S(1)}, bf16[256,640]{1,0:T(8,128)(2,1)S(1)}, u32[]{:S(2)}, u32[]{:S(2)}) collective-permute-start(bf16[256,640]{1,0:T(8,128)(2,1)S(1)} %slice.34.refs_0_), channel_id=1, source_target_pairs={{0,8},{1,25},{8,16},{9,1},{16,24},{17,9},{24,0},{25,17},{2,10},{3,... | collective-permute-start | bytes 983048 | tf_op jit(solution)/shard_map/ppermute | solution.py:185
  76.9 0.0 copy-start.1
  76.9 1.2 collective-permute-start.5
  78.1 11.8 %collective-permute-done.refs_1_ = bf16[256,640]{1,0:T(8,128)(2,1)S(1)} collective-permute-done((bf16[256,640]{1,0:T(8,128)(2,1)S(1)}, bf16[256,640]{1,0:T(8,128)(2,1)S(1)}, u32[]{:S(2)}, u32[]{:S(2)}) %collective-permute-start) | collective-permute-done | bytes 327712 | tf_op jit(solution)/shard_map/ppermute | solution.py:185
  90.0 3.1 %collective-permute-start.1 = (bf16[256,640]{1,0:T(8,128)(2,1)S(1)}, bf16[256,640]{1,0:T(8,128)(2,1)S(1)}, u32[]{:S(2)}, u32[]{:S(2)}) collective-permute-start(bf16[256,640]{1,0:T(8,128)(2,1)S(1)} %collective-permute-done.refs_1_), channel_id=1, source_target_pairs={{0,8},{1,25},{8,16},{9,1},{16,24},{17,9},{24,0},{25,17},{2,10},{3,... | collective-permute-start | bytes 983048 | tf_op jit(solution)/shard_map/ppermute | solution.py:185
  93.0 7.2 %collective-permute-done.5.refs_5_ = bf16[256,640]{1,0:T(8,128)(2,1)S(1)} collective-permute-done((bf16[256,640]{1,0:T(8,128)(2,1)S(1)}, bf16[256,640]{1,0:T(8,128)(2,1)S(1)}, u32[]{:S(2)}, u32[]{:S(2)}) %collective-permute-start.5) | collective-permute-done | bytes 327712 | tf_op jit(solution)/shard_map/ppermute | solution.py:185
  100.2 3.1 %collective-permute-start.6 = (bf16[256,640]{1,0:T(8,128)(2,1)S(1)}, bf16[256,640]{1,0:T(8,128)(2,1)S(1)}, u32[]{:S(2)}, u32[]{:S(2)}) collective-permute-start(bf16[256,640]{1,0:T(8,128)(2,1)S(1)} %collective-permute-done.5.refs_5_), channel_id=1, source_target_pairs={{0,8},{1,25},{8,16},{9,1},{16,24},{17,9},{24,0},{25,17},{2,10},{3,... | collective-permute-start | bytes 983048 | tf_op jit(solution)/shard_map/ppermute | solution.py:185
  103.2 7.1 %collective-permute-done.1.refs_2_ = bf16[256,640]{1,0:T(8,128)(2,1)S(1)} collective-permute-done((bf16[256,640]{1,0:T(8,128)(2,1)S(1)}, bf16[256,640]{1,0:T(8,128)(2,1)S(1)}, u32[]{:S(2)}, u32[]{:S(2)}) %collective-permute-start.1) | collective-permute-done | bytes 327712 | tf_op jit(solution)/shard_map/ppermute | solution.py:185
  110.4 3.1 %collective-permute-start.10 = (bf16[256,640]{1,0:T(8,128)(2,1)S(1)}, bf16[256,640]{1,0:T(8,128)(2,1)S(1)}, u32[]{:S(2)}, u32[]{:S(2)}) collective-permute-start(bf16[256,640]{1,0:T(8,128)(2,1)S(1)} %collective-permute-done.1.refs_2_), channel_id=1, source_target_pairs={{0,8},{1,25},{8,16},{9,1},{16,24},{17,9},{24,0},{25,17},{2,10},{3,... | collective-permute-start | bytes 983048 | tf_op jit(solution)/shard_map/ppermute | solution.py:185
  113.5 0.4 collective-permute-done.6.refs_6_
  113.9 3.1 %collective-permute-start.11 = (bf16[256,640]{1,0:T(8,128)(2,1)S(1)}, bf16[256,640]{1,0:T(8,128)(2,1)S(1)}, u32[]{:S(2)}, u32[]{:S(2)}) collective-permute-start(bf16[256,640]{1,0:T(8,128)(2,1)S(1)} %collective-permute-done.6.refs_6_), channel_id=1, source_target_pairs={{0,8},{1,25},{8,16},{9,1},{16,24},{17,9},{24,0},{25,17},{2,10},{3,... | collective-permute-start | bytes 983048 | tf_op jit(solution)/shard_map/ppermute | solution.py:185
  117.0 2.3 %collective-permute-start.7 = (bf16[256,256]{1,0:T(8,128)(2,1)S(1)}, bf16[256,256]{1,0:T(8,128)(2,1)S(1)}, u32[]{:S(2)}, u32[]{:S(2)}) collective-permute-start(bf16[256,256]{1,0:T(8,128)(2,1)S(1)} %slice.36.refs_4_), channel_id=1, source_target_pairs={{0,8},{1,25},{8,16},{9,1},{16,24},{17,9},{24,0},{25,17},{2,10},{3,... | collective-permute-start | bytes 393224 | tf_op jit(solution)/shard_map/ppermute | solution.py:185
  119.4 1.5 collective-permute-start.2
  120.8 0.6 stack.35.place
  121.5 0.0 collective-permute-done.10.refs_3_
  121.5 0.5 collective-permute-done.11.refs_7_
  122.0 0.2 copy-done.8
  122.2 0.5 copy-done.9
  122.7 9.6 %shard_map.97 = bf16[8,192,640]{2,1,0:T(8,128)(2,1)} custom-call(s32[8]{0:T(128)} %stack.35.place, bf16[1536,2048]{1,0:T(8,128)(2,1)} %all-gather.2.cloned.1.call-done.tokens, bf16[256,640]{1,0:T(8,128)(2,1)} %copy-done, bf16[256,640]{1,0:T(8,128)(2,1)} %copy-done.4, bf16[256,640]{1,0:T(8,128)(2,1)} %copy-done.6, bf16[256,640]{1,0:T(8,128)(2,1)} %copy-done.8, ...), custom_call_target="tpu_custom_call" | custom-call | flops 1 | bytes 1 | tf_op jit(solution)/shard_map/pallas_call | solution.py:132
  132.2 0.0 copy-done.2
  132.2 0.0 collective-permute-done.7.refs_5_
  132.2 0.0 copy-start.10
  132.3 0.0 collective-permute-done.2.refs_1_
  132.3 3.6 %all-to-all-start.4 = ((bf16[8,192,640]{2,1,0:T(8,128)(2,1)}), bf16[8,192,640]{2,1,0:T(8,128)(2,1)S(1)}, u32[]{:S(2)}, u32[]{:S(2)}) async-start(bf16[8,192,640]{2,1,0:T(8,128)(2,1)} %shard_map.97), calls=%async_computation.4 | async-start | bytes 3932160 | tf_op jit(solution)/shard_map/all_to_all | solution.py:230
  135.8 0.0 copy-done.10
  135.9 3.4 %collective-permute-start.8 = (bf16[256,256]{1,0:T(8,128)(2,1)S(1)}, bf16[256,256]{1,0:T(8,128)(2,1)S(1)}, u32[]{:S(2)}, u32[]{:S(2)}) collective-permute-start(bf16[256,256]{1,0:T(8,128)(2,1)S(1)} %collective-permute-done.7.refs_5_), channel_id=1, source_target_pairs={{0,8},{1,25},{8,16},{9,1},{16,24},{17,9},{24,0},{25,17},{2,10},{3,... | collective-permute-start | bytes 393224 | tf_op jit(solution)/shard_map/ppermute | solution.py:185
  139.2 1.8 collective-permute-start.3
  141.0 2.5 %collective-permute-done.8.refs_6_ = bf16[256,256]{1,0:T(8,128)(2,1)S(1)} collective-permute-done((bf16[256,256]{1,0:T(8,128)(2,1)S(1)}, bf16[256,256]{1,0:T(8,128)(2,1)S(1)}, u32[]{:S(2)}, u32[]{:S(2)}) %collective-permute-start.8) | collective-permute-done | bytes 131104 | tf_op jit(solution)/shard_map/ppermute | solution.py:185
  143.5 2.0 %collective-permute-start.9 = (bf16[256,256]{1,0:T(8,128)(2,1)S(1)}, bf16[256,256]{1,0:T(8,128)(2,1)S(1)}, u32[]{:S(2)}, u32[]{:S(2)}) collective-permute-start(bf16[256,256]{1,0:T(8,128)(2,1)S(1)} %collective-permute-done.8.refs_6_), channel_id=1, source_target_pairs={{0,8},{1,25},{8,16},{9,1},{16,24},{17,9},{24,0},{25,17},{2,10},{3,... | collective-permute-start | bytes 393224 | tf_op jit(solution)/shard_map/ppermute | solution.py:185
  145.5 0.0 collective-permute-done.3.refs_2_
  145.5 2.6 %collective-permute-start.4 = (bf16[256,256]{1,0:T(8,128)(2,1)S(1)}, bf16[256,256]{1,0:T(8,128)(2,1)S(1)}, u32[]{:S(2)}, u32[]{:S(2)}) collective-permute-start(bf16[256,256]{1,0:T(8,128)(2,1)S(1)} %collective-permute-done.3.refs_2_), channel_id=1, source_target_pairs={{0,8},{1,25},{8,16},{9,1},{16,24},{17,9},{24,0},{25,17},{2,10},{3,... | collective-permute-start | bytes 393224 | tf_op jit(solution)/shard_map/ppermute | solution.py:185
  148.1 1.5 collective-permute-done.9.refs_7_
  149.6 2.7 %collective-permute-done.4.refs_3_ = bf16[256,256]{1,0:T(8,128)(2,1)S(1)} collective-permute-done((bf16[256,256]{1,0:T(8,128)(2,1)S(1)}, bf16[256,256]{1,0:T(8,128)(2,1)S(1)}, u32[]{:S(2)}, u32[]{:S(2)}) %collective-permute-start.4) | collective-permute-done | bytes 131104 | tf_op jit(solution)/shard_map/ppermute | solution.py:185
  152.3 0.6 copy-done.15
  152.9 6.4 %shard_map.96 = bf16[8,192,256]{2,1,0:T(8,128)(2,1)} custom-call(s32[8]{0:T(128)} %stack.35.place, bf16[1536,2048]{1,0:T(8,128)(2,1)} %all-gather.2.cloned.1.call-done.tokens, bf16[256,256]{1,0:T(8,128)(2,1)} %copy-done.3, bf16[256,256]{1,0:T(8,128)(2,1)} %copy-done.11, bf16[256,256]{1,0:T(8,128)(2,1)} %copy-done.13, bf16[256,256]{1,0:T(8,128)(2,1)} %copy-done.15, ...), custom_call_target="tpu_custom_call" | custom-call | flops 1 | bytes 1 | tf_op jit(solution)/shard_map/pallas_call | solution.py:132
  159.3 1.0 all-to-all-done.4.part
  160.3 5.6 %all-to-all-start.3 = ((bf16[8,192,256]{2,1,0:T(8,128)(2,1)}), bf16[8,192,256]{2,1,0:T(8,128)(2,1)S(1)}, u32[]{:S(2)}, u32[]{:S(2)}) async-start(bf16[8,192,256]{2,1,0:T(8,128)(2,1)} %shard_map.96), calls=%async_computation.3 | async-start | bytes 1572864 | tf_op jit(solution)/shard_map/all_to_all | solution.py:232
  165.9 1.6 shard_map.98.refs_0_
  167.5 10.7 %all-to-all-done.3.part = bf16[8,192,256]{2,1,0:T(8,128)(2,1)S(1)} async-done(((bf16[8,192,256]{2,1,0:T(8,128)(2,1)}), bf16[8,192,256]{2,1,0:T(8,128)(2,1)S(1)}, u32[]{:S(2)}, u32[]{:S(2)}) %all-to-all-start.3) | async-done | bytes 786464 | tf_op jit(solution)/shard_map/all_to_all | solution.py:232
  178.2 1.0 shard_map.99
  (30 shorter events, 0.1 us)
Async XLA Ops:
  7.2 114.8 %all-gather.2.cloned.1.call-start = ((), (), s32[]{:S(2)}) async-start(), calls=%async_computation.5 | async-start | bytes 7077888 | tf_op jit(solution)/shard_map/all_gather | solution.py:219
  71.6 50.3 %copy-start = (bf16[256,640]{1,0:T(8,128)(2,1)}, bf16[256,640]{1,0:T(8,128)(2,1)S(1)}, u32[]{:S(2)}) copy-start(bf16[256,640]{1,0:T(8,128)(2,1)S(1)} %slice.34.refs_0_) | copy-start | bytes 983044
  71.6 18.3 %collective-permute-start = (bf16[256,640]{1,0:T(8,128)(2,1)S(1)}, bf16[256,640]{1,0:T(8,128)(2,1)S(1)}, u32[]{:S(2)}, u32[]{:S(2)}) collective-permute-start(bf16[256,640]{1,0:T(8,128)(2,1)S(1)} %slice.34.refs_0_), channel_id=1, source_target_pairs={{0,8},{1,25},{8,16},{9,1},{16,24},{17,9},{24,0},{25,17},{2,10},{3,... | collective-permute-start | bytes 983048 | tf_op jit(solution)/shard_map/ppermute | solution.py:185
  76.9 45.1 %copy-start.1 = (bf16[256,640]{1,0:T(8,128)(2,1)}, bf16[256,640]{1,0:T(8,128)(2,1)S(1)}, u32[]{:S(2)}) copy-start(bf16[256,640]{1,0:T(8,128)(2,1)S(1)} %slice.37.refs_4_) | copy-start | bytes 983044
  76.9 23.3 %collective-permute-start.5 = (bf16[256,640]{1,0:T(8,128)(2,1)S(1)}, bf16[256,640]{1,0:T(8,128)(2,1)S(1)}, u32[]{:S(2)}, u32[]{:S(2)}) collective-permute-start(bf16[256,640]{1,0:T(8,128)(2,1)S(1)} %slice.37.refs_4_), channel_id=1, source_target_pairs={{0,8},{1,25},{8,16},{9,1},{16,24},{17,9},{24,0},{25,17},{2,10},{3,... | collective-permute-start | bytes 983048 | tf_op jit(solution)/shard_map/ppermute | solution.py:185
  90.0 32.0 %copy-start.4 = (bf16[256,640]{1,0:T(8,128)(2,1)}, bf16[256,640]{1,0:T(8,128)(2,1)S(1)}, u32[]{:S(2)}) copy-start(bf16[256,640]{1,0:T(8,128)(2,1)S(1)} %collective-permute-done.refs_1_) | copy-start | bytes 983044
  90.0 20.4 %collective-permute-start.1 = (bf16[256,640]{1,0:T(8,128)(2,1)S(1)}, bf16[256,640]{1,0:T(8,128)(2,1)S(1)}, u32[]{:S(2)}, u32[]{:S(2)}) collective-permute-start(bf16[256,640]{1,0:T(8,128)(2,1)S(1)} %collective-permute-done.refs_1_), channel_id=1, source_target_pairs={{0,8},{1,25},{8,16},{9,1},{16,24},{17,9},{24,0},{25,17},{2,10},{3,... | collective-permute-start | bytes 983048 | tf_op jit(solution)/shard_map/ppermute | solution.py:185
  100.2 21.8 %copy-start.5 = (bf16[256,640]{1,0:T(8,128)(2,1)}, bf16[256,640]{1,0:T(8,128)(2,1)S(1)}, u32[]{:S(2)}) copy-start(bf16[256,640]{1,0:T(8,128)(2,1)S(1)} %collective-permute-done.5.refs_5_) | copy-start | bytes 983044
  100.2 13.7 %collective-permute-start.6 = (bf16[256,640]{1,0:T(8,128)(2,1)S(1)}, bf16[256,640]{1,0:T(8,128)(2,1)S(1)}, u32[]{:S(2)}, u32[]{:S(2)}) collective-permute-start(bf16[256,640]{1,0:T(8,128)(2,1)S(1)} %collective-permute-done.5.refs_5_), channel_id=1, source_target_pairs={{0,8},{1,25},{8,16},{9,1},{16,24},{17,9},{24,0},{25,17},{2,10},{3,... | collective-permute-start | bytes 983048 | tf_op jit(solution)/shard_map/ppermute | solution.py:185
  110.4 11.6 %copy-start.6 = (bf16[256,640]{1,0:T(8,128)(2,1)}, bf16[256,640]{1,0:T(8,128)(2,1)S(1)}, u32[]{:S(2)}) copy-start(bf16[256,640]{1,0:T(8,128)(2,1)S(1)} %collective-permute-done.1.refs_2_) | copy-start | bytes 983044
  110.4 11.1 %collective-permute-start.10 = (bf16[256,640]{1,0:T(8,128)(2,1)S(1)}, bf16[256,640]{1,0:T(8,128)(2,1)S(1)}, u32[]{:S(2)}, u32[]{:S(2)}) collective-permute-start(bf16[256,640]{1,0:T(8,128)(2,1)S(1)} %collective-permute-done.1.refs_2_), channel_id=1, source_target_pairs={{0,8},{1,25},{8,16},{9,1},{16,24},{17,9},{24,0},{25,17},{2,10},{3,... | collective-permute-start | bytes 983048 | tf_op jit(solution)/shard_map/ppermute | solution.py:185
  113.9 8.1 %copy-start.7 = (bf16[256,640]{1,0:T(8,128)(2,1)}, bf16[256,640]{1,0:T(8,128)(2,1)S(1)}, u32[]{:S(2)}) copy-start(bf16[256,640]{1,0:T(8,128)(2,1)S(1)} %collective-permute-done.6.refs_6_) | copy-start | bytes 983044
  113.9 8.0 %collective-permute-start.11 = (bf16[256,640]{1,0:T(8,128)(2,1)S(1)}, bf16[256,640]{1,0:T(8,128)(2,1)S(1)}, u32[]{:S(2)}, u32[]{:S(2)}) collective-permute-start(bf16[256,640]{1,0:T(8,128)(2,1)S(1)} %collective-permute-done.6.refs_6_), channel_id=1, source_target_pairs={{0,8},{1,25},{8,16},{9,1},{16,24},{17,9},{24,0},{25,17},{2,10},{3,... | collective-permute-start | bytes 983048 | tf_op jit(solution)/shard_map/ppermute | solution.py:185
  117.0 15.2 %copy-start.2 = (bf16[256,256]{1,0:T(8,128)(2,1)}, bf16[256,256]{1,0:T(8,128)(2,1)S(1)}, u32[]{:S(2)}) copy-start(bf16[256,256]{1,0:T(8,128)(2,1)S(1)} %slice.36.refs_4_) | copy-start | bytes 393220
  117.0 15.2 %copy-start.3 = (bf16[256,256]{1,0:T(8,128)(2,1)}, bf16[256,256]{1,0:T(8,128)(2,1)S(1)}, u32[]{:S(2)}) copy-start(bf16[256,256]{1,0:T(8,128)(2,1)S(1)} %slice.33.refs_0_) | copy-start | bytes 393220
  117.0 15.2 %collective-permute-start.7 = (bf16[256,256]{1,0:T(8,128)(2,1)S(1)}, bf16[256,256]{1,0:T(8,128)(2,1)S(1)}, u32[]{:S(2)}, u32[]{:S(2)}) collective-permute-start(bf16[256,256]{1,0:T(8,128)(2,1)S(1)} %slice.36.refs_4_), channel_id=1, source_target_pairs={{0,8},{1,25},{8,16},{9,1},{16,24},{17,9},{24,0},{25,17},{2,10},{3,... | collective-permute-start | bytes 393224 | tf_op jit(solution)/shard_map/ppermute | solution.py:185
  119.4 12.9 %collective-permute-start.2 = (bf16[256,256]{1,0:T(8,128)(2,1)S(1)}, bf16[256,256]{1,0:T(8,128)(2,1)S(1)}, u32[]{:S(2)}, u32[]{:S(2)}) collective-permute-start(bf16[256,256]{1,0:T(8,128)(2,1)S(1)} %slice.33.refs_0_), channel_id=1, source_target_pairs={{0,8},{1,25},{8,16},{9,1},{16,24},{17,9},{24,0},{25,17},{2,10},{3,... | collective-permute-start | bytes 393224 | tf_op jit(solution)/shard_map/ppermute | solution.py:185
  121.5 0.8 copy-start.8
  121.9 0.8 copy-start.9
  132.2 3.6 %copy-start.10 = (bf16[256,256]{1,0:T(8,128)(2,1)}, bf16[256,256]{1,0:T(8,128)(2,1)S(1)}, u32[]{:S(2)}) copy-start(bf16[256,256]{1,0:T(8,128)(2,1)S(1)} %collective-permute-done.7.refs_5_) | copy-start | bytes 393220
  132.3 7.0 %copy-start.11 = (bf16[256,256]{1,0:T(8,128)(2,1)}, bf16[256,256]{1,0:T(8,128)(2,1)S(1)}, u32[]{:S(2)}) copy-start(bf16[256,256]{1,0:T(8,128)(2,1)S(1)} %collective-permute-done.2.refs_1_) | copy-start | bytes 393220
  132.3 28.0 %all-to-all-start.4 = ((bf16[8,192,640]{2,1,0:T(8,128)(2,1)}), bf16[8,192,640]{2,1,0:T(8,128)(2,1)S(1)}, u32[]{:S(2)}, u32[]{:S(2)}) async-start(bf16[8,192,640]{2,1,0:T(8,128)(2,1)} %shard_map.97), calls=%async_computation.4 | async-start | bytes 3932160 | tf_op jit(solution)/shard_map/all_to_all | solution.py:230
  135.9 7.6 %collective-permute-start.8 = (bf16[256,256]{1,0:T(8,128)(2,1)S(1)}, bf16[256,256]{1,0:T(8,128)(2,1)S(1)}, u32[]{:S(2)}, u32[]{:S(2)}) collective-permute-start(bf16[256,256]{1,0:T(8,128)(2,1)S(1)} %collective-permute-done.7.refs_5_), channel_id=1, source_target_pairs={{0,8},{1,25},{8,16},{9,1},{16,24},{17,9},{24,0},{25,17},{2,10},{3,... | collective-permute-start | bytes 393224 | tf_op jit(solution)/shard_map/ppermute | solution.py:185
  139.2 6.2 %collective-permute-start.3 = (bf16[256,256]{1,0:T(8,128)(2,1)S(1)}, bf16[256,256]{1,0:T(8,128)(2,1)S(1)}, u32[]{:S(2)}, u32[]{:S(2)}) collective-permute-start(bf16[256,256]{1,0:T(8,128)(2,1)S(1)} %collective-permute-done.2.refs_1_), channel_id=1, source_target_pairs={{0,8},{1,25},{8,16},{9,1},{16,24},{17,9},{24,0},{25,17},{2,10},{3,... | collective-permute-start | bytes 393224 | tf_op jit(solution)/shard_map/ppermute | solution.py:185
  143.5 8.8 %copy-start.12 = (bf16[256,256]{1,0:T(8,128)(2,1)}, bf16[256,256]{1,0:T(8,128)(2,1)S(1)}, u32[]{:S(2)}) copy-start(bf16[256,256]{1,0:T(8,128)(2,1)S(1)} %collective-permute-done.8.refs_6_) | copy-start | bytes 393220
  143.5 6.1 %collective-permute-start.9 = (bf16[256,256]{1,0:T(8,128)(2,1)S(1)}, bf16[256,256]{1,0:T(8,128)(2,1)S(1)}, u32[]{:S(2)}, u32[]{:S(2)}) collective-permute-start(bf16[256,256]{1,0:T(8,128)(2,1)S(1)} %collective-permute-done.8.refs_6_), channel_id=1, source_target_pairs={{0,8},{1,25},{8,16},{9,1},{16,24},{17,9},{24,0},{25,17},{2,10},{3,... | collective-permute-start | bytes 393224 | tf_op jit(solution)/shard_map/ppermute | solution.py:185
  145.5 6.8 %copy-start.13 = (bf16[256,256]{1,0:T(8,128)(2,1)}, bf16[256,256]{1,0:T(8,128)(2,1)S(1)}, u32[]{:S(2)}) copy-start(bf16[256,256]{1,0:T(8,128)(2,1)S(1)} %collective-permute-done.3.refs_2_) | copy-start | bytes 393220
  145.5 6.8 %collective-permute-start.4 = (bf16[256,256]{1,0:T(8,128)(2,1)S(1)}, bf16[256,256]{1,0:T(8,128)(2,1)S(1)}, u32[]{:S(2)}, u32[]{:S(2)}) collective-permute-start(bf16[256,256]{1,0:T(8,128)(2,1)S(1)} %collective-permute-done.3.refs_2_), channel_id=1, source_target_pairs={{0,8},{1,25},{8,16},{9,1},{16,24},{17,9},{24,0},{25,17},{2,10},{3,... | collective-permute-start | bytes 393224 | tf_op jit(solution)/shard_map/ppermute | solution.py:185
  149.6 2.7 %copy-start.14 = (bf16[256,256]{1,0:T(8,128)(2,1)}, bf16[256,256]{1,0:T(8,128)(2,1)S(1)}, u32[]{:S(2)}) copy-start(bf16[256,256]{1,0:T(8,128)(2,1)S(1)} %collective-permute-done.9.refs_7_) | copy-start | bytes 393220
  152.3 0.7 copy-start.15
  160.3 17.9 %all-to-all-start.3 = ((bf16[8,192,256]{2,1,0:T(8,128)(2,1)}), bf16[8,192,256]{2,1,0:T(8,128)(2,1)S(1)}, u32[]{:S(2)}, u32[]{:S(2)}) async-start(bf16[8,192,256]{2,1,0:T(8,128)(2,1)} %shard_map.96), calls=%async_computation.3 | async-start | bytes 1572864 | tf_op jit(solution)/shard_map/all_to_all | solution.py:232
Sparse Core Ops, SparseCore 0:
  9.8 47.6 all-gather.1
